TPU v7x, 32 devices: a whole 2x2x4 slice. The times are simulated.
32 devices in a mesh: pipe: 2 (over core), seq: 4 (over y, x), tensor: 4 (over z).
Axes of the slice: x: 2, y: 2, z: 4, core: 2. Of those that a mesh axis runs over, the one named last changes fastest.
Arguments:
- token_ids: int32 [2, 768], P(None, 'seq'), may hold values from 0 to 511
- embed_table: bfloat16 [512, 8192], P(None, 'tensor'), may hold values from -24 to 24
- in_proj: bfloat16 [2, 8192, 3, 4096], P('pipe', None, None, 'tensor'), may hold values from -0.0625 to 0.0625
- feat_taps: float32 [2, 3, 3, 4096], P('pipe', None, None, 'tensor'), may hold values from -3 to 3
- se_taps: float32 [7, 4096], P(None, 'tensor'), may hold values from -2 to 2
- mr_taps: float32 [128, 4096], P(None, 'tensor'), may hold values from -0.6 to 0.6
- out_proj: bfloat16 [2, 4096, 8192], P('pipe', 'tensor'), may hold values from -0.125 to 0.125
- norm_gain: bfloat16 [2, 8192], P('pipe', 'tensor'), may hold values from 0.25 to 1.75
Outputs:
- segment_out: bfloat16 [2, 2, 768, 8192], P('pipe', None, 'seq', 'tensor')
All inputs are finite; a program needn't handle non-finite values.
Results may differ from a plain program's by a relative error of at most 0.023.
Values may be sent and summed in bfloat16 or wider, within the bound.
A program may use at most 192 MiB of HBM per device.

v0:
```python
import jax
import jax.numpy as jnp
from jax import lax
from jax.sharding import PartitionSpec as P

VOCAB = 512
KL = 128
KS = 7
KF = 3
SEGMENTS = 2
HALO = 129


epsilon = 1e-06


def from_behind(value, axis, steps):
    count = lax.axis_size(axis)
    pairs = [(source, (source + steps) % count) for source in range(count)]
    return lax.ppermute(value, axis, pairs)


def passed_along(value, axis, steps):
    count = lax.axis_size(axis)
    first, last = (max(0, -steps), min(count, count - steps))
    return lax.ppermute(value, axis, [(source, source + steps) for source in range(first, last)])


def project(stream, w_flat, gain_cols):
    gathered, gain_all = (
        lax.all_gather(stream, "tensor", axis=2, tiled=True),
        lax.all_gather(gain_cols, "tensor", axis=1, tiled=True),
    )
    values = gathered.astype(jnp.float32)
    inv_rms = lax.rsqrt(jnp.mean(values * values, axis=2, keepdims=True) + epsilon)
    normed = (values * inv_rms * gain_all[0].astype(jnp.float32)).astype(jnp.bfloat16)
    projected = jnp.einsum("snd,dk->snk", normed, w_flat, preferred_element_type=jnp.float32)
    return projected.astype(jnp.bfloat16)


def send_tails(projected):
    row_count = projected.shape[1]
    chan_local = projected.shape[2] // 3
    kv_tail = projected[:, row_count - HALO :, chan_local:]
    q_tail = projected[:, row_count - (KF - 1) :, :chan_local]
    return from_behind((kv_tail, q_tail), "seq", 1)


def hand_over(result):
    return passed_along(result, "pipe", 1)


def mixing(stream, projected, kv_prev, q_prev, feat_local, long_taps, w_down):
    row_count = projected.shape[1]
    chan_local = projected.shape[2] // 3
    q_all = jnp.concatenate([q_prev, projected[:, :, :chan_local]], axis=1).astype(jnp.float32)
    kv_all = jnp.concatenate([kv_prev, projected[:, :, chan_local:]], axis=1).astype(jnp.float32)
    q_taps = feat_local[0, :, 0, :]
    kv_taps = feat_local[0, :, 1:, :].reshape(KF, 2 * chan_local)
    kv_span = KL - 1 + row_count
    q_feat = jnp.zeros((projected.shape[0], row_count, chan_local), jnp.float32)
    kv_feat = jnp.zeros((projected.shape[0], kv_span, 2 * chan_local), jnp.float32)
    for tap_index in range(KF):
        offset = KF - 1 - tap_index
        q_feat = q_feat + q_taps[tap_index] * q_all[:, offset : offset + row_count]
        kv_feat = kv_feat + kv_taps[tap_index] * kv_all[:, offset : offset + kv_span]
    gated_kv = kv_feat[:, :, :chan_local] * kv_feat[:, :, chan_local:]

    def add_tap(tap_index, running):
        shifted = lax.dynamic_slice_in_dim(gated_kv, KL - 1 - tap_index, row_count, 1)
        return running + long_taps[tap_index] * shifted

    filtered = lax.fori_loop(0, KL, add_tap, jnp.zeros_like(q_feat))
    y_out = (q_feat * filtered).astype(jnp.bfloat16)
    partial_terms = jnp.einsum("snc,cd->snd", y_out, w_down[0], preferred_element_type=jnp.float32)
    mixed = lax.psum_scatter(
        partial_terms.astype(jnp.bfloat16), "tensor", scatter_dimension=2, tiled=True
    ).astype(jnp.float32)
    return (stream.astype(jnp.float32) + mixed).astype(jnp.bfloat16)


def local(token_ids, embed_table, in_proj, feat_taps, se_taps, mr_taps, out_proj, norm_gain):
    section = lax.axis_index("pipe")
    shard_pos = lax.axis_index("seq")
    lead_segment = section == 0
    padded_se = jnp.concatenate(
        [se_taps, jnp.zeros((KL - KS, se_taps.shape[1]), jnp.float32)], axis=0
    )
    long_taps = jnp.where(lead_segment, padded_se, mr_taps)
    w_flat = in_proj[0].reshape(in_proj.shape[1], -1)
    vocab_ids = jnp.arange(VOCAB, dtype=jnp.int32)
    one_hot = (token_ids[:, :, None] == vocab_ids[None, None, :]).astype(jnp.bfloat16)
    embedded = jnp.einsum(
        "snv,vd->snd", one_hot, embed_table, preferred_element_type=jnp.float32
    ).astype(jnp.bfloat16)
    current = jnp.where(lead_segment, embedded, jnp.zeros_like(embedded))
    outputs = []
    for step_index in range(SEGMENTS):
        projected = project(current, w_flat, norm_gain)
        kv_recv, q_recv = send_tails(projected)
        kv_earlier = jnp.concatenate([jnp.zeros_like(kv_recv[:1]), kv_recv[:-1]], axis=0)
        q_earlier = jnp.concatenate([jnp.zeros_like(q_recv[:1]), q_recv[:-1]], axis=0)
        kv_prev = jnp.where(shard_pos == 0, kv_earlier, kv_recv)
        q_prev = jnp.where(shard_pos == 0, q_earlier, q_recv)
        result = mixing(current, projected, kv_prev, q_prev, feat_taps, long_taps, out_proj)
        outputs.append(result)
        if step_index + 1 < SEGMENTS:
            current = hand_over(result)
    final_out = lax.dynamic_index_in_dim(jnp.stack(outputs, axis=0), section, 0, keepdims=True)
    return final_out


def solution(mesh):
    return jax.shard_map(
        local,
        mesh=mesh,
        in_specs=(
            P(None, "seq"),
            P(None, "tensor"),
            P("pipe", None, None, "tensor"),
            P("pipe", None, None, "tensor"),
            P(None, "tensor"),
            P(None, "tensor"),
            P("pipe", "tensor", None),
            P("pipe", "tensor"),
        ),
        out_specs=P("pipe", None, "seq", "tensor"),
        check_vma=False,
    )
```

profile of v0, /device:TPU:25, one launch (start us, length us, event | category | flops | bytes accessed | tf_op | source)
XLA Modules:
  0.0 1215.7 jit_solution(5998731246950927160)
XLA Ops:
  8.1 2.9 fusion.34
  11.1 62.4 %copy.12 = bf16[1,8192,3,1024]{1,3,2,0:T(8,128)(2,1)} copy(bf16[1,8192,3,1024]{3,1,2,0:T(8,128)(2,1)} %param.14) | data formatting | bytes 100663296 | tf_op args[2]
  73.4 13.4 %all_gather.11 = bf16[1,8192]{1,0:T(2,128)(2,1)S(1)} all-gather(bf16[1,2048]{1,0:T(2,128)(2,1)S(1)} %copy-done.9), channel_id=1, replica_groups=mesh['pipe'=2,'seq'=4,'tensor'=4] {'tensor'}, dimensions={1}, use_global_device_ids=true | all-gather | bytes 20480 | tf_op jit(solution)/shard_map/all_gather | solution.py:32
  86.9 38.2 %all-gather.3.cloned.1.call-done = bf16[2,192,8192]{2,1,0:T(8,128)(2,1)} async-done(((bf16[2,192,2048]{2,1,0:T(8,128)(2,1)}), bf16[2,192,8192]{2,1,0:T(8,128)(2,1)}) %all-gather.3.cloned.1.call-update) | async-done | bytes 6291472 | tf_op jit(solution)/shard_map/all_gather | solution.py:31
  125.1 4.1 fusion.4
  129.2 27.6 %fusion.28 = bf16[2,192,3072]{2,1,0:T(8,128)(2,1)} fusion(bf16[8192,3072,1]{0,1,2:T(8,128)(2,1)} %bitcast.37, bf16[2,192,8192]{2,1,0:T(8,128)(2,1)} %all-gather.3.cloned.1.call-done, f32[8192]{0:T(1024)S(1)} %bitcast.50, f32[2,192]{1,0:T(2,128)S(1)} %add_rsqrt_fusion.1), kind=kOutput, calls=%fused_computation.36 | convolution fusion | flops 19341115392 | bytes 59016704 | tf_op jit(solution)/shard_map/snd,dk->snk/dot_general | solution.py:37
  163.6 22.7 %collective-permute-done = bf16[2,2,1024]{2,1,0:T(2,128)(2,1)S(1)} collective-permute-done((bf16[2,2,1024]{2,1,0:T(2,128)(2,1)S(1)}, bf16[2,2,1024]{2,1,0:T(2,128)(2,1)S(1)}, u32[]{:S(2)}, u32[]{:S(2)}) %collective-permute-start) | collective-permute-done | bytes 8224 | tf_op jit(solution)/shard_map/ppermute | solution.py:20
  193.6 283.8 %while.32 = (s32[]{:T(128)}, f32[2,192,1024]{2,1,0:T(8,128)S(1)}, f32[128,1024]{1,0:T(8,128)S(1)}, f32[2,319,1024]{2,1,0:T(8,128)}, s32[]{:T(128)}, /*index=5*/s32[]{:T(128)}, s32[]{:T(128)}, s32[]{:T(128)}) while((s32[]{:T(128)}, f32[2,192,1024]{2,1,0:T(8,128)S(1)}, f32[128,1024]{1,0:T(8,128)S(1)}, f32[2,319,1024]{2,1,0:T(8,128)}, ...), condition=%wide.region_2.3_spmd.clone, body=%wide.region_1.2_spmd.clone.sunk | while | flops 1179655 | bytes 4731029 | solution.py:73
  195.8 2.2 select_add_fusion.4
  206.9 2.2 select_add_fusion.4
  211.3 2.2 select_add_fusion.4
  218.0 2.2 select_add_fusion.4
  222.4 2.2 select_add_fusion.4
  233.5 2.2 select_add_fusion.4
  237.9 2.2 select_add_fusion.4
  249.0 2.2 select_add_fusion.4
  253.5 2.2 select_add_fusion.4
  260.1 2.2 select_add_fusion.4
  264.6 2.2 select_add_fusion.4
  275.6 2.2 select_add_fusion.4
  477.4 15.6 %fusion.10 = bf16[2,192,8192]{2,1,0:T(8,128)(2,1)} fusion(bf16[1,1024,8192]{2,1,0:T(8,128)(2,1)} %param.18, f32[2,192,1024]{2,1,0:T(8,128)S(1)} %get-tuple-element.225, f32[2,194,1024]{2,1,0:T(8,128)} %maximum_convert_fusion.2, f32[1024]{0:T(1024)S(1)} %bitcast.54, f32[1024]{0:T(1024)S(1)} %bitcast.56, f32[1024]{0:T(1024)S(1)} %bitcast.52), kind=kOutput, calls=%fused_computation.18 | convolution fusion | flops 6448349184 | bytes 29372416 | tf_op jit(solution)/shard_map/snc,cd->snd/dot_general | solution.py:75
  493.0 111.3 %reduce-scatter.3.cloned.1.call-done = bf16[2,192,2048]{2,1,0:T(8,128)(2,1)} async-done(((bf16[2,192,8192]{2,1,0:T(8,128)(2,1)}), bf16[2,192,2048]{2,1,0:T(8,128)(2,1)}) %reduce-scatter.3.cloned.1.call-update) | async-done | bytes 1572880 | tf_op jit(solution)/shard_map/reduce_scatter | solution.py:76
  604.4 2.5 add_convert_fusion.1
  608.2 4.1 collective-permute-done.2
  612.7 113.0 %all-gather.5.cloned.1.call-done = bf16[2,192,8192]{2,1,0:T(8,128)(2,1)} async-done(((bf16[2,192,2048]{2,1,0:T(8,128)(2,1)}), bf16[2,192,8192]{2,1,0:T(8,128)(2,1)}) %all-gather.5.cloned.1.call-update) | async-done | bytes 6291472 | tf_op jit(solution)/shard_map/all_gather | solution.py:31
  725.6 4.1 fusion.7
  729.8 27.6 %fusion.31 = bf16[2,192,3072]{2,1,0:T(8,128)(2,1)} fusion(bf16[8192,3072,1]{0,1,2:T(8,128)(2,1)} %bitcast.38, bf16[2,192,8192]{2,1,0:T(8,128)(2,1)} %all-gather.5.cloned.1.call-done, f32[2,192]{1,0:T(2,128)S(1)} %add_rsqrt_fusion, f32[8192]{0:T(1024)S(1)} %bitcast.51), kind=kOutput, calls=%fused_computation.37 | convolution fusion | flops 19341115392 | bytes 59016704 | tf_op jit(solution)/shard_map/snd,dk->snk/dot_general | solution.py:37
  764.1 22.7 %collective-permute-done.3 = bf16[2,2,1024]{2,1,0:T(2,128)(2,1)S(1)} collective-permute-done((bf16[2,2,1024]{2,1,0:T(2,128)(2,1)S(1)}, bf16[2,2,1024]{2,1,0:T(2,128)(2,1)S(1)}, u32[]{:S(2)}, u32[]{:S(2)}) %collective-permute-start.3) | collective-permute-done | bytes 8224 | tf_op jit(solution)/shard_map/ppermute | solution.py:20
  794.1 283.8 %while.33 = (s32[]{:T(128)}, f32[2,192,1024]{2,1,0:T(8,128)S(1)}, f32[128,1024]{1,0:T(8,128)S(1)}, f32[2,319,1024]{2,1,0:T(8,128)}, s32[]{:T(128)}, /*index=5*/s32[]{:T(128)}, s32[]{:T(128)}, s32[]{:T(128)}) while((s32[]{:T(128)}, f32[2,192,1024]{2,1,0:T(8,128)S(1)}, f32[128,1024]{1,0:T(8,128)S(1)}, f32[2,319,1024]{2,1,0:T(8,128)}, ...), condition=%wide.region_6.7_spmd.clone, body=%wide.region_5.6_spmd.clone.sunk | while | flops 1179655 | bytes 4731029 | solution.py:73
  1077.9 15.6 %fusion.13 = bf16[2,192,8192]{2,1,0:T(8,128)(2,1)} fusion(bf16[1,1024,8192]{2,1,0:T(8,128)(2,1)} %param.18, f32[2,192,1024]{2,1,0:T(8,128)S(1)} %get-tuple-element.226, f32[2,194,1024]{2,1,0:T(8,128)} %maximum_convert_fusion.3, f32[1024]{0:T(1024)S(1)} %bitcast.55, f32[1024]{0:T(1024)S(1)} %bitcast.57, f32[1024]{0:T(1024)S(1)} %bitcast.53), kind=kOutput, calls=%fused_computation.19 | convolution fusion | flops 6448349184 | bytes 29372416 | tf_op jit(solution)/shard_map/snc,cd->snd/dot_general | solution.py:75
  1093.5 111.3 %reduce-scatter.5.cloned.1.call-done = bf16[2,192,2048]{2,1,0:T(8,128)(2,1)} async-done(((bf16[2,192,8192]{2,1,0:T(8,128)(2,1)}), bf16[2,192,2048]{2,1,0:T(8,128)(2,1)}) %reduce-scatter.5.cloned.1.call-update) | async-done | bytes 1572880 | tf_op jit(solution)/shard_map/reduce_scatter | solution.py:76
  1204.9 2.6 fusion.36
  (574 shorter events, 565.4 us)
Async XLA Ops:
  6.5 1.6 copy-start
  6.5 118.6 %all-gather.3.cloned.1.call-start = ((), (), s32[]{:S(2)}) async-start(), calls=%async_computation.2 | async-start | bytes 7864320 | tf_op jit(solution)/shard_map/all_gather | solution.py:31
  11.0 62.4 %copy-start.9 = (bf16[1,2048]{1,0:T(2,128)(2,1)S(1)}, bf16[1,2048]{1,0:T(2,128)(2,1)}, u32[]{:S(2)}) copy-start(bf16[1,2048]{1,0:T(2,128)(2,1)} %param.19) | copy-start | bytes 12292
  11.0 593.4 %reduce-scatter.3.cloned.1.call-start = ((), (), s32[]{:S(2)}) async-start(), calls=%async_computation.3 | async-start | bytes 7864320 | tf_op jit(solution)/shard_map/reduce_scatter | solution.py:76
  156.8 5.2 copy-start.7
  156.8 5.3 copy-start.6
  156.8 5.3 copy-start.8
  156.8 5.3 copy-start.4
  160.6 27.2 %collective-permute-start.1 = (bf16[2,129,2048]{2,0,1:T(2,128)(2,1)}, bf16[2,129,2048]{2,0,1:T(2,128)(2,1)S(1)}, u32[]{:S(2)}, u32[]{:S(2)}) collective-permute-start(bf16[2,129,2048]{2,0,1:T(2,128)(2,1)} %copy.14), channel_id=1, source_target_pairs={{0,4},{4,8},{8,12},{12,0},{1,5},{5,9},{9,13},{13,1},{2,6},{6,10},{... | collective-permute-start | bytes 3170312 | tf_op jit(solution)/shard_map/ppermute | solution.py:20
  162.1 24.1 %collective-permute-start = (bf16[2,2,1024]{2,1,0:T(2,128)(2,1)S(1)}, bf16[2,2,1024]{2,1,0:T(2,128)(2,1)S(1)}, u32[]{:S(2)}, u32[]{:S(2)}) collective-permute-start(bf16[2,2,1024]{2,1,0:T(2,128)(2,1)S(1)} %slice.158), channel_id=1, source_target_pairs={{0,4},{4,8},{8,12},{12,0},{1,5},{5,9},{9,13},{13,1},{2,6},{6,10},{... | collective-permute-start | bytes 24584 | tf_op jit(solution)/shard_map/ppermute | solution.py:20
  163.6 22.8 %slice-start.1 = ((bf16[2,192,3072]{2,1,0:T(8,128)(2,1)}), bf16[2,192,1024]{2,1,0:T(8,128)(2,1)S(1)}, s32[]{:S(2)}) async-start(bf16[2,192,3072]{2,1,0:T(8,128)(2,1)} %fusion.28), calls=%async_computation.7 | async-start | bytes 1572864 | tf_op jit(solution)/shard_map/slice | solution.py:56
  187.8 1.4 slice-start
  493.0 232.6 %all-gather.5.cloned.1.call-start = ((), (), s32[]{:S(2)}) async-start(), calls=%async_computation.4 | async-start | bytes 7864320 | tf_op jit(solution)/shard_map/all_gather | solution.py:31
  606.9 122.8 %copy-start.2 = (bf16[2,192,2048]{2,1,0:T(8,128)(2,1)}, bf16[2,192,2048]{2,1,0:T(8,128)(2,1)S(1)}, u32[]{:S(2)}) copy-start(bf16[2,192,2048]{2,1,0:T(8,128)(2,1)S(1)} %add_convert_fusion.1) | copy-start | bytes 4718596
  606.9 5.4 collective-permute-start.2
  612.4 592.5 %reduce-scatter.5.cloned.1.call-start = ((), (), s32[]{:S(2)}) async-start(), calls=%async_computation.5 | async-start | bytes 7864320 | tf_op jit(solution)/shard_map/reduce_scatter | solution.py:76
  757.4 5.2 copy-start.5
  761.1 27.1 %collective-permute-start.4 = (bf16[2,129,2048]{2,0,1:T(2,128)(2,1)}, bf16[2,129,2048]{2,0,1:T(2,128)(2,1)S(1)}, u32[]{:S(2)}, u32[]{:S(2)}) collective-permute-start(bf16[2,129,2048]{2,0,1:T(2,128)(2,1)} %copy.18), channel_id=1, source_target_pairs={{0,4},{4,8},{8,12},{12,0},{1,5},{5,9},{9,13},{13,1},{2,6},{6,10},{... | collective-permute-start | bytes 3170312 | tf_op jit(solution)/shard_map/ppermute | solution.py:20
  762.6 24.2 %collective-permute-start.3 = (bf16[2,2,1024]{2,1,0:T(2,128)(2,1)S(1)}, bf16[2,2,1024]{2,1,0:T(2,128)(2,1)S(1)}, u32[]{:S(2)}, u32[]{:S(2)}) collective-permute-start(bf16[2,2,1024]{2,1,0:T(2,128)(2,1)S(1)} %slice.172), channel_id=1, source_target_pairs={{0,4},{4,8},{8,12},{12,0},{1,5},{5,9},{9,13},{13,1},{2,6},{6,10},{... | collective-permute-start | bytes 24584 | tf_op jit(solution)/shard_map/ppermute | solution.py:20
  764.1 22.8 %slice-start.2 = ((bf16[2,192,3072]{2,1,0:T(8,128)(2,1)}), bf16[2,192,1024]{2,1,0:T(8,128)(2,1)S(1)}, s32[]{:S(2)}) async-start(bf16[2,192,3072]{2,1,0:T(8,128)(2,1)} %fusion.31), calls=%async_computation.8 | async-start | bytes 1572864 | tf_op jit(solution)/shard_map/slice | solution.py:56
  788.3 1.4 slice-start.3
  1204.9 2.6 copy-start.3
  1207.5 1.7 copy-start.1
Sparse Core Ops, SparseCore 0:
  11.1 113.9 all-gather.2
  493.1 111.2 reduce-scatter.2
  612.5 113.0 all-gather.4
  1093.6 111.1 reduce-scatter.4
where the time goes:
time: 1230 us; the launch traced here: 1220 us
  other arithmetic  584 us (47%)
  waiting for transfers between devices  424 us (34%)
  matrix products  89.2 us (7%)
  local copies, waits for them, and re-layouts  75.8 us (6%)
  blocking collectives  13.4 us (1%)
  between operations  13.4 us (1%)
    add x256, other arithmetic, add_tap(): return running + long_taps[tap_index] * shifted  556 us
    reduce_scatter x2, waiting for transfers between devices, mixing(): lax.psum_scatter(partial_terms.astype(jnp.bfloat16), 'tensor', scatter_di...  223 us
    all_gather x2, waiting for transfers between devices, project(): lax.all_gather(stream, 'tensor', axis=2, tiled=True)  151 us
    unnamed x23, local copies, waits for them, and re-layouts  64.6 us
    dot_general x2, matrix products, project(): jnp.einsum('snd,dk->snk', normed, w_flat, preferred_element_type=jnp.floa...  55.2 us
    ppermute x4, waiting for transfers between devices, from_behind(): return lax.ppermute(value, axis, pairs)  45.5 us
    dot_general x2, matrix products, mixing(): jnp.einsum('snc,cd->snd', y_out, w_down[0], preferred_element_type=jnp.fl...  31.2 us
  transfers between devices with their start and end apart: 9, of which 7 were waited for; matrix products, arithmetic and copies ran while one was open for 5% of the time, Pallas kernels for 0%

commit v1 on v0

v1 whole, which is shorter than its diff:
```python
import functools

import jax
import jax.numpy as jnp
from jax import lax
from jax.experimental import pallas as pl
from jax.experimental.pallas import tpu as pltpu
from jax.sharding import PartitionSpec as P

KL = 128
KS = 7
KF = 3
HEAD = 16
TAPS_AT_ONCE = 4
VMEM_LIMIT = 50 * 1024 * 1024


epsilon = 1e-06


def pairs_on(section, axis, links):
    count = lax.axis_size(axis)
    base = section * count
    return [(base + source, base + target) for source, target in links]


def send_on(value, section, axis, links):
    return lax.ppermute(value, ("pipe", axis), pairs_on(section, axis, links))


def gather_features(block, section):
    count = lax.axis_size("tensor")
    if count > 4:
        return lax.all_gather(block, "tensor", axis=0)
    place = lax.axis_index("tensor")
    up, down = [block], [block]
    for step in range(1, count):
        up.append(send_on(up[-1], section, "tensor", [(i, i + 1) for i in range(step - 1, count - 1)]))
        down.append(send_on(down[-1], section, "tensor", [(i, i - 1) for i in range(1, count - step + 1)]))
    whole = []
    for owner in range(count):
        value = block
        for step in range(1, count - owner):
            value = jnp.where(place == owner + step, up[step], value)
        for step in range(1, owner + 1):
            value = jnp.where(place == owner - step, down[step], value)
        whole.append(value)
    return jnp.stack(whole, axis=0)


def scatter_sum(partial, section):
    count = lax.axis_size("tensor")
    place = lax.axis_index("tensor")
    if count > 4:
        own = lax.psum_scatter(partial, "tensor", scatter_dimension=2, tiled=False)
        return own.astype(jnp.float32)

    def block(index):
        index = jnp.clip(index, 0, count - 1)
        return lax.dynamic_index_in_dim(partial, index, 2, keepdims=False).astype(jnp.float32)

    up = down = None
    for step in range(1, count):
        up_block = block(count - step + place)
        down_block = block(step - count + place)
        if step > 1:
            up_block = up_block + up.astype(jnp.float32)
            down_block = down_block + down.astype(jnp.float32)
        up = send_on(up_block.astype(jnp.bfloat16), section, "tensor", [(i, i + 1) for i in range(step)])
        down = send_on(
            down_block.astype(jnp.bfloat16), section, "tensor", [(i, i - 1) for i in range(count - step, count)]
        )
    total = block(place)
    if up is not None:
        total = total + up.astype(jnp.float32) + down.astype(jnp.float32)
    return total


def project_kernel(x_ref, w_ref, inv_ref, out_ref, total):
    step = pl.program_id(1)

    @pl.when(step == 0)
    def _():
        total[...] = jnp.zeros_like(total)

    total[...] += jnp.dot(x_ref[0], w_ref[0], preferred_element_type=jnp.float32)

    @pl.when(step == pl.num_programs(1) - 1)
    def _():
        out_ref[...] = (total[...] * inv_ref[...]).astype(out_ref.dtype)


def project(gathered, weights, inv_rms):
    count, rows, width = gathered.shape
    groups, depth, channels = weights.shape
    tile = min(width, 1024)
    per_block = width // tile
    return pl.pallas_call(
        project_kernel,
        grid=(groups, depth // tile),
        in_specs=[
            pl.BlockSpec((1, rows, tile), lambda g, k: (k // per_block, 0, k % per_block)),
            pl.BlockSpec((1, tile, channels), lambda g, k: (g, k, 0)),
            pl.BlockSpec((rows, 1), lambda g, k: (0, 0)),
        ],
        out_specs=pl.BlockSpec((rows, channels), lambda g, k: (0, g)),
        out_shape=jax.ShapeDtypeStruct((rows, groups * channels), jnp.bfloat16),
        scratch_shapes=[pltpu.VMEM((rows, channels), jnp.float32)],
        compiler_params=pltpu.CompilerParams(vmem_limit_bytes=VMEM_LIMIT),
        cost_estimate=pl.CostEstimate(
            flops=2 * rows * depth * groups * channels,
            bytes_accessed=2 * (groups * depth * channels + rows * depth),
            transcendentals=0,
        ),
    )(gathered, weights, inv_rms)


def mix_kernel(taps_count, has_history, *refs):
    if has_history:
        q_ref, k_ref, v_ref, history_ref, feat_ref, taps_ref, out_ref, wide, gated, shifted = refs
    else:
        q_ref, k_ref, v_ref, feat_ref, taps_ref, out_ref, wide, gated, shifted = refs
    rows = out_ref.shape[1]
    span = KL + rows

    def featured(ref, which, back):
        wide[...] = ref[0].astype(jnp.float32)
        value = jnp.zeros((back + rows, wide.shape[1]), jnp.float32)
        for tap in range(KF):
            value = value + feat_ref[tap, which : which + 1, :] * wide[
                HEAD - back - tap : HEAD - tap + rows, :
            ]
        return value

    back = 0 if has_history else 8
    gated[KL - back :, :] = featured(k_ref, 1, back) * featured(v_ref, 2, back)
    if has_history:
        gated[:KL, :] = history_ref[0].astype(jnp.float32)
    phases = min(8, taps_count)
    for phase in range(phases):
        start = 8 if has_history else KL
        shifted[phase, start:, :] = gated[start - phase : span - phase, :]

    lanes = out_ref.shape[2]
    if taps_count <= 8:
        total = jnp.zeros((rows, lanes), jnp.float32)
        for phase in range(phases):
            total = total + taps_ref[phase : phase + 1, :] * shifted[phase, KL:, :]
    else:

        def body(step, total):
            base = pl.multiple_of(step * (8 * TAPS_AT_ONCE), 8 * TAPS_AT_ONCE)
            taps = taps_ref[pl.ds(base, 8 * TAPS_AT_ONCE), :]
            start = pl.multiple_of(KL - 8 * (TAPS_AT_ONCE - 1) - base, 8)
            for phase in range(8):
                window = shifted[phase, pl.ds(start, rows + 8 * (TAPS_AT_ONCE - 1)), :]
                for late in range(TAPS_AT_ONCE):
                    offset = 8 * (TAPS_AT_ONCE - 1 - late)
                    tap = 8 * late + phase
                    total = total + taps[tap : tap + 1, :] * window[offset : offset + rows, :]
            return total

        total = lax.fori_loop(
            0, taps_count // (8 * TAPS_AT_ONCE), body, jnp.zeros((rows, lanes), jnp.float32)
        )
    out_ref[0] = (featured(q_ref, 0, 0) * total).astype(out_ref.dtype)


def mix(extended, history, feat_taps, taps):
    slices, length, wide_channels = extended.shape
    channels = wide_channels // 3
    rows = length - HEAD
    lanes = 128
    blocks = channels // lanes
    in_specs = [
        pl.BlockSpec((1, length, lanes), functools.partial(lambda g, s, c: (s, 0, g * blocks + c), g))
        for g in range(3)
    ]
    operands = [extended, extended, extended]
    if history is not None:
        in_specs.append(pl.BlockSpec((1, KL, lanes), lambda s, c: (s, 0, c)))
        operands.append(history)
    in_specs.append(pl.BlockSpec((KF, 3, lanes), lambda s, c: (0, 0, c)))
    in_specs.append(pl.BlockSpec((taps.shape[0], lanes), lambda s, c: (0, c)))
    operands += [feat_taps, taps]
    return pl.pallas_call(
        functools.partial(mix_kernel, taps.shape[0], history is not None),
        grid=(slices, blocks),
        in_specs=in_specs,
        out_specs=pl.BlockSpec((1, rows, lanes), lambda s, c: (s, 0, c)),
        out_shape=jax.ShapeDtypeStruct((slices, rows, channels), jnp.bfloat16),
        scratch_shapes=[
            pltpu.VMEM((length, lanes), jnp.float32),
            pltpu.VMEM((KL + rows, lanes), jnp.float32),
            pltpu.VMEM((8, KL + rows, lanes), jnp.float32),
        ],
        compiler_params=pltpu.CompilerParams(vmem_limit_bytes=VMEM_LIMIT),
        cost_estimate=pl.CostEstimate(
            flops=2 * taps.shape[0] * slices * rows * channels,
            bytes_accessed=2 * slices * length * 4 * channels,
            transcendentals=0,
        ),
    )(*operands)


def after_previous(received, shard_pos, fill):
    earlier = jnp.concatenate([jnp.full_like(received[:1], fill), received[:-1]], axis=0)
    return jnp.where(shard_pos == 0, earlier, received)


def inverse_rms(values):
    width = values.shape[-1] * lax.axis_size("tensor")
    squares = lax.psum(jnp.sum(values * values, axis=-1, keepdims=True), "tensor")
    return lax.rsqrt(squares / width + epsilon)


def finish(stream, y_out, w_down, section):
    count = lax.axis_size("tensor")
    slices, rows, _ = y_out.shape
    partial = jnp.einsum("snc,cd->snd", y_out, w_down, preferred_element_type=jnp.float32)
    partial = partial.astype(jnp.bfloat16).reshape(slices, rows, count, -1)
    mixed = scatter_sum(partial, section)
    return (stream.astype(jnp.float32) + mixed).astype(jnp.bfloat16)


def one_hot(ids, vocab):
    return (ids[..., None] == jnp.arange(vocab, dtype=jnp.int32)).astype(jnp.bfloat16)


def local(token_ids, embed_table, in_proj, feat_taps, se_taps, mr_taps, out_proj, norm_gain):
    section = lax.axis_index("pipe")
    shard_pos = lax.axis_index("seq")
    shards = lax.axis_size("seq")
    vocab, width = embed_table.shape
    slices, rows = token_ids.shape
    weights = jnp.transpose(in_proj[0], (1, 0, 2))
    gain = norm_gain.astype(jnp.float32)
    ring = [(i, (i + 1) % shards) for i in range(shards)]

    share = vocab // shards
    own_rows = lax.dynamic_slice_in_dim(embed_table, shard_pos * share, share, 0).astype(jnp.float32)
    scaled = gather_features((own_rows * gain).astype(jnp.bfloat16), 0)
    own_table = project(scaled, weights, inverse_rms(own_rows))
    tables = [own_table]
    for step in range(1, shards):
        tables.append(send_on(own_table, 0, "seq", [(i, i ^ step) for i in range(shards)]))
    table = jnp.concatenate(tables, axis=0)
    prev_ids = after_previous(send_on(token_ids[:, rows - HEAD :], 0, "seq", ring), shard_pos, -1)
    ids = jnp.concatenate([prev_ids, token_ids], axis=1)
    moved = jnp.where(ids < 0, -1, ((ids // share) ^ shard_pos) * share + ids % share)
    extended = jnp.einsum(
        "snv,vc->snc", one_hot(moved, vocab), table, preferred_element_type=jnp.float32
    ).astype(jnp.bfloat16)
    embedded = jnp.einsum(
        "snv,vd->snd", one_hot(token_ids, vocab), embed_table, preferred_element_type=jnp.float32
    ).astype(jnp.bfloat16)
    y_out = mix(extended, None, feat_taps[0], se_taps)
    first = finish(embedded, y_out, out_proj[0], 0)

    stream = lax.ppermute(first, "pipe", [(0, 1)])
    values = stream.reshape(slices * rows, width).astype(jnp.float32)
    scaled = gather_features((values * gain).astype(jnp.bfloat16), 1)
    projected = project(scaled, weights, inverse_rms(values)).reshape(slices, rows, -1)
    channels = projected.shape[2] // 3
    tail = projected[:, rows - HEAD :, :]
    late = projected[:, rows - KL - KF + 1 :, channels:].astype(jnp.float32)
    kv_taps = feat_taps[0, :, 1:, :].reshape(KF, 2 * channels)
    kv_feat = sum(kv_taps[tap] * late[:, KF - 1 - tap : KF - 1 - tap + KL] for tap in range(KF))
    gated_tail = (kv_feat[:, :, :channels] * kv_feat[:, :, channels:]).astype(jnp.bfloat16)
    history = after_previous(send_on(gated_tail, 1, "seq", ring), shard_pos, 0)
    head = after_previous(send_on(tail, 1, "seq", ring), shard_pos, 0)
    extended = jnp.concatenate([head, projected], axis=1)
    y_out = mix(extended, history, feat_taps[0], mr_taps)
    second = finish(stream, y_out, out_proj[0], 1)
    return jnp.where(section == 0, first, second)[None]


def solution(mesh):
    return jax.shard_map(
        local,
        mesh=mesh,
        in_specs=(
            P(None, "seq"),
            P(None, "tensor"),
            P("pipe", None, None, "tensor"),
            P("pipe", None, None, "tensor"),
            P(None, "tensor"),
            P(None, "tensor"),
            P("pipe", "tensor", None),
            P("pipe", "tensor"),
        ),
        out_specs=P("pipe", None, "seq", "tensor"),
        check_vma=False,
    )
```

time: 1230 us -> 552 us (0.45)
  other arithmetic: 584 us -> 38.4 us
  waiting for transfers between devices: 424 us -> 206 us
  Pallas kernels: 0 us -> 89.3 us
  matrix products: 89.2 us -> 31.6 us
  starting transfers between devices: 7.44 us -> 44.9 us
  blocking collectives: 13.4 us -> 42.3 us
  local copies, waits for them, and re-layouts: 75.8 us -> 93.6 us
  between operations: 13.4 us -> 0.97 us
    add x258 -> x1, other arithmetic: 559 us -> 0.62 us  [local(): sum((kv_taps[tap] * late[:, KF - 1 - tap:KF - 1 - tap + KL] for tap in ra...]
    reduce_scatter x2 -> x0, waiting for transfers between devices: 223 us -> none  [mixing(): lax.psum_scatter(partial_terms.astype(jnp.bfloat16), 'tensor', scatter_di...]
    ppermute x5 -> x31, waiting for transfers between devices: 49.6 us -> 206 us  [the longest x1 112 us: local(): stream = lax.ppermute(first, 'pipe', [(0, 1)])]
    all_gather x2 -> x0, waiting for transfers between devices: 151 us -> none  [project(): lax.all_gather(stream, 'tensor', axis=2, tiled=True)]
    pallas_call x0 -> x4, Pallas kernels: none -> 89.3 us  [the longest x2 65 us: project(): pl.pallas_call(project_kernel, grid=(groups, depth // tile), in_specs=[pl...]
    dynamic_slice x256 -> x2, local copies, waits for them, and re-layouts: 2.82 us -> 65.7 us  [block(): lax.dynamic_index_in_dim(partial, index, 2, keepdims=False)]
    unnamed x23 -> x19, local copies, waits for them, and re-layouts: 64.6 us -> 4.99 us
    dot_general x5 -> x4, matrix products: 89.2 us -> 31.6 us  [the longest x2 28.7 us: finish(): jnp.einsum('snc,cd->snd', y_out, w_down, preferred_element_type=jnp.float32)]
  transfers between devices with their start and end apart: 9 -> 31, of which waited for: 7 -> 10; matrix products, arithmetic and copies ran while one was open for 5% -> 4% of each run, Pallas kernels for 0% -> 0%
where the time goes in v1:
time: 552 us; the launch traced here: 547 us
  waiting for transfers between devices  206 us (37%)
  local copies, waits for them, and re-layouts  93.6 us (17%)
  Pallas kernels  89.3 us (16%)
  starting transfers between devices  44.9 us (8%)
  blocking collectives  42.3 us (8%)
  other arithmetic  38.4 us (7%)
  matrix products  31.6 us (6%)
    ppermute x1, waiting for transfers between devices, local(): stream = lax.ppermute(first, 'pipe', [(0, 1)])  112 us
    ppermute x30, waiting for transfers between devices, send_on(): return lax.ppermute(value, ('pipe', axis), pairs_on(section, axis, links))  93.6 us
    dynamic_slice x2, local copies, waits for them, and re-layouts, block(): lax.dynamic_index_in_dim(partial, index, 2, keepdims=False)  65.7 us
    pallas_call x2, Pallas kernels, project(): pl.pallas_call(project_kernel, grid=(groups, depth // tile), in_specs=[pl...  65 us
    ppermute x30, starting transfers between devices, send_on(): return lax.ppermute(value, ('pipe', axis), pairs_on(section, axis, links))  43.6 us
    psum x2, blocking collectives, inverse_rms(): lax.psum(jnp.sum(values * values, axis=-1, keepdims=True), 'tensor')  42.3 us
    dot_general x2, matrix products, finish(): jnp.einsum('snc,cd->snd', y_out, w_down, preferred_element_type=jnp.float32)  28.7 us
    pallas_call x2, Pallas kernels, mix(): pl.pallas_call(functools.partial(mix_kernel, taps.shape[0], history is no...  24.3 us
  transfers between devices with their start and end apart: 31, of which 10 were waited for; matrix products, arithmetic and copies ran while one was open for 4% of the time, Pallas kernels for 0%

profile of v1, /device:TPU:25, one launch (start us, length us, event | category | flops | bytes accessed | tf_op | source)
XLA Modules:
  0.0 546.9 jit_solution(801107725012669872)
XLA Ops:
  7.1 13.1 %psum.14 = f32[128,1]{1,0:T(8,128)S(1)} all-reduce(f32[128,1]{1,0:T(8,128)S(1)} %copy.34), channel_id=1, replica_groups=mesh['pipe'=2,'seq'=4,'tensor'=4] {'tensor'}, use_global_device_ids=true, to_apply=%region_1.2 | all-reduce | flops 128 | bytes 1024 | tf_op jit(solution)/shard_map/psum | solution.py:213
  21.8 27.9 %shard_map.82 = bf16[128,3072]{1,0:T(8,128)(2,1)S(1)} custom-call(bf16[4,128,2048]{2,1,0:T(8,128)(2,1)S(1)} %pad_maximum_fusion.2.x_ref, bf16[3,8192,1024]{2,1,0:T(8,128)(2,1)} %bitcast.121, f32[128,1]{1,0:T(8,128)S(1)} %add_rsqrt_fusion.1.inv_ref), custom_call_target="tpu_custom_call" | custom-call | flops 6442450944 | bytes 52428800 | tf_op jit(solution)/shard_map/pallas_call | solution.py:98
  54.8 3.7 shard_map.83
  58.5 14.4 %fusion.4 = bf16[2,192,8192]{2,1,0:T(8,128)(2,1)} fusion(bf16[2,192,1024]{2,1,0:T(8,128)(2,1)S(1)} %shard_map.83, bf16[1,1024,8192]{2,1,0:T(8,128)(2,1)} %param.14), kind=kOutput, calls=%fused_computation.4 | convolution fusion | flops 6445596672 | bytes 23855104 | tf_op jit(solution)/shard_map/snc,cd->snd/dot_general | solution.py:220
  72.9 11.2 %reshape.160 = bf16[2,192,4,2048]{3,2,1,0:T(4,128)(2,1)} reshape(bf16[2,192,8192]{2,1,0:T(8,128)(2,1)} %fusion.4) | data formatting | bytes 12582912 | tf_op jit(solution)/shard_map/reshape | solution.py:221
  84.1 32.5 %constant_dynamic-slice_fusion.13 = (bf16[2,192,1,2048]{3,2,1,0:T(2,128)(2,1)S(1)}, bf16[2,192,1,2048]{3,2,1,0:T(2,128)(2,1)S(1)}, bf16[2,192,1,2048]{3,2,1,0:T(...) fusion(bf16[2,192,4,2048]{3,2,1,0:T(4,128)(2,1)} %reshape.160, ...), kind=kLoop, calls=%fused_computation.106 | loop fusion | bytes 22020124 | tf_op jit(solution)/shard_map/jit(dynamic_index_in_dim)/dynamic_slice | solution.py:60
  131.5 2.1 fusion.29
  135.0 112.3 %collective-permute-done.16 = bf16[2,192,2048]{2,1,0:T(8,128)(2,1)S(1)} collective-permute-done((bf16[2,192,2048]{2,1,0:T(8,128)(2,1)S(1)}, bf16[2,192,2048]{2,1,0:T(8,128)(2,1)S(1)}, u32[]{:S(2)}, u32[]{:S(2)}) %collective-permute-start.16) | collective-permute-done | bytes 1572896 | tf_op jit(solution)/shard_map/ppermute | solution.py:260
  250.8 16.8 %collective-permute-done.20 = bf16[384,2048]{1,0:T(8,128)(2,1)S(1)} collective-permute-done((bf16[384,2048]{1,0:T(8,128)(2,1)S(1)}, bf16[384,2048]{1,0:T(8,128)(2,1)S(1)}, u32[]{:S(2)}, u32[]{:S(2)}) %collective-permute-start.20) | collective-permute-done | bytes 1572896 | tf_op jit(solution)/shard_map/ppermute | solution.py:28
  270.6 2.0 collective-permute-done.17
  275.8 18.3 %collective-permute-done.18 = bf16[384,2048]{1,0:T(8,128)(2,1)} collective-permute-done((bf16[384,2048]{1,0:T(8,128)(2,1)S(1)}, bf16[384,2048]{1,0:T(8,128)(2,1)}, u32[]{:S(2)}, u32[]{:S(2)}) %collective-permute-start.18) | collective-permute-done | bytes 1572896 | tf_op jit(solution)/shard_map/ppermute | solution.py:28
  296.1 29.3 %psum.15 = f32[384,1]{1,0:T(8,128)} all-reduce(f32[384,1]{1,0:T(8,128)S(1)} %broadcast_in_dim.23), channel_id=1, replica_groups=mesh['pipe'=2,'seq'=4,'tensor'=4] {'tensor'}, use_global_device_ids=true, to_apply=%region_3.4 | all-reduce | flops 384 | bytes 3072 | tf_op jit(solution)/shard_map/psum | solution.py:213
  326.3 3.8 select_bitcast_fusion.3
  330.1 3.2 pad_maximum_fusion.x_ref
  333.4 37.1 %shard_map.84 = bf16[384,3072]{1,0:T(8,128)(2,1)S(1)} custom-call(bf16[4,384,2048]{2,1,0:T(8,128)(2,1)} %pad_maximum_fusion.x_ref, bf16[3,8192,1024]{2,1,0:T(8,128)(2,1)} %bitcast.122, f32[384,1]{1,0:T(8,128)S(1)} %add_rsqrt_fusion.inv_ref), custom_call_target="tpu_custom_call" | custom-call | flops 19327352832 | bytes 56623104 | tf_op jit(solution)/shard_map/pallas_call | solution.py:98
  370.8 3.2 collective-permute-start.23
  374.8 3.0 collective-permute-start.24
  379.8 5.8 %collective-permute-done.24 = bf16[2,128,1024]{2,1,0:T(8,128)(2,1)S(1)} collective-permute-done((bf16[2,128,1024]{2,1,0:T(8,128)(2,1)S(1)}, bf16[2,128,1024]{2,1,0:T(8,128)(2,1)S(1)}, u32[]{:S(2)}, u32[]{:S(2)}) %collective-permute-start.24) | collective-permute-done | bytes 524320 | tf_op jit(solution)/shard_map/ppermute | solution.py:28
  385.7 20.6 %shard_map.85 = bf16[2,192,1024]{2,1,0:T(8,128)(2,1)S(1)} custom-call(bf16[2,208,3072]{2,1,0:T(8,128)(2,1)} %pad_maximum_fusion.1.refs_0_.refs_1_.refs_2_, bf16[2,208,3072]{2,1,0:T(8,128)(2,1)} %pad_maximum_fusion.1.refs_0_.refs_1_.refs_2_, bf16[2,208,3072]{2,1,0:T(8,128)(2,1)} %pad_maximum_fusion.1.refs_0_.refs_1_.refs_2_, ...), custom_call_target="tpu_custom_call" | custom-call | flops 100663296 | bytes 3407872 | tf_op jit(solution)/shard_map/pallas_call | solution.py:186
  406.3 14.4 %fusion.7 = bf16[2,192,8192]{2,1,0:T(8,128)(2,1)} fusion(bf16[2,192,1024]{2,1,0:T(8,128)(2,1)S(1)} %shard_map.85, bf16[1,1024,8192]{2,1,0:T(8,128)(2,1)} %param.14), kind=kOutput, calls=%fused_computation.5 | convolution fusion | flops 6445596672 | bytes 23855104 | tf_op jit(solution)/shard_map/snc,cd->snd/dot_general | solution.py:220
  420.7 11.2 %reshape.162 = bf16[2,192,4,2048]{3,2,1,0:T(4,128)(2,1)} reshape(bf16[2,192,8192]{2,1,0:T(8,128)(2,1)} %fusion.7) | data formatting | bytes 12582912 | tf_op jit(solution)/shard_map/reshape | solution.py:221
  431.9 33.3 %constant_dynamic-slice_fusion.6 = (bf16[2,192,1,2048]{3,2,1,0:T(2,128)(2,1)}, bf16[2,192,1,2048]{3,2,1,0:T(2,128)(2,1)S(1)}, bf16[2,192,1,2048]{3,2,1,0:T(2,128...) fusion(bf16[2,192,4,2048]{3,2,1,0:T(4,128)(2,1)} %reshape.162, ...), kind=kLoop, calls=%fused_computation.99 | loop fusion | bytes 22020124 | tf_op jit(solution)/shard_map/jit(dynamic_index_in_dim)/dynamic_slice | solution.py:60
  466.1 3.3 collective-permute-start.28
  471.3 15.3 %collective-permute-done.28 = bf16[2,192,2048]{2,1,0:T(8,128)(2,1)S(1)} collective-permute-done((bf16[2,192,2048]{2,1,0:T(8,128)(2,1)S(1)}, bf16[2,192,2048]{2,1,0:T(8,128)(2,1)S(1)}, u32[]{:S(2)}, u32[]{:S(2)}) %collective-permute-start.28) | collective-permute-done | bytes 1572896 | tf_op jit(solution)/shard_map/ppermute | solution.py:28
  488.3 3.9 collective-permute-start.29
  494.8 14.7 %collective-permute-done.29 = bf16[2,192,2048]{2,1,0:T(8,128)(2,1)S(1)} collective-permute-done((bf16[2,192,2048]{2,1,0:T(8,128)(2,1)S(1)}, bf16[2,192,2048]{2,1,0:T(8,128)(2,1)S(1)}, u32[]{:S(2)}, u32[]{:S(2)}) %collective-permute-start.29) | collective-permute-done | bytes 1572896 | tf_op jit(solution)/shard_map/ppermute | solution.py:28
  509.5 2.3 fusion.17
  511.8 5.0 collective-permute-start.30
  516.8 2.3 fusion.19
  520.4 12.8 %collective-permute-done.30 = bf16[2,192,2048]{2,1,0:T(8,128)(2,1)} collective-permute-done((bf16[2,192,2048]{2,1,0:T(8,128)(2,1)}, bf16[2,192,2048]{2,1,0:T(8,128)(2,1)}, u32[]{:S(2)}, u32[]{:S(2)}) %collective-permute-start.30) | collective-permute-done | bytes 1572896 | tf_op jit(solution)/shard_map/ppermute | solution.py:28
  533.3 7.3 %collective-permute-done.27 = bf16[2,192,2048]{2,1,0:T(8,128)(2,1)} collective-permute-done((bf16[2,192,2048]{2,1,0:T(8,128)(2,1)}, bf16[2,192,2048]{2,1,0:T(8,128)(2,1)}, u32[]{:S(2)}, u32[]{:S(2)}) %collective-permute-start.27) | collective-permute-done | bytes 1572896 | tf_op jit(solution)/shard_map/ppermute | solution.py:28
  540.6 6.1 %fusion.35 = bf16[1,2,192,2048]{3,2,1,0:T(8,128)(2,1)} fusion(bf16[2,192,2048]{2,1,0:T(8,128)(2,1)S(1)} %fusion.29, bf16[2,192,2048]{2,1,0:T(8,128)(2,1)} %collective-permute-done.30, bf16[2,192,2048]{2,1,0:T(8,128)(2,1)} %collective-permute-done.27, bf16[2,192,1,2048]{3,2,1,0:T(2,128)(2,1)} %get-tuple-element.5, ...), kind=kLoop, calls=%fused_computation.52 | loop fusion | flops 7077888 | bytes 9437185 | tf_op jit(solution)/shard_map/broadcast_in_dim | solution.py:275
  (99 shorter events, 53.6 us)
Async XLA Ops:
  2.0 1.4 collective-permute-start.4
  2.7 1.4 collective-permute-start.1
  3.4 1.4 collective-permute-start.5
  4.1 1.4 collective-permute-start.2
  4.8 15.4 %collective-permute-start.6 = (bf16[128,2048]{1,0:T(8,128)(2,1)S(1)}, bf16[128,2048]{1,0:T(8,128)(2,1)S(1)}, u32[]{:S(2)}, u32[]{:S(2)}) collective-permute-start(bf16[128,2048]{1,0:T(8,128)(2,1)S(1)} %collective-permute-done.5), channel_id=1, source_target_pairs={{1,0},{5,4},{9,8},{13,12}} | collective-permute-start | bytes 1572872 | tf_op jit(solution)/shard_map/ppermute | solution.py:28
  5.5 14.7 %collective-permute-start.3 = (bf16[128,2048]{1,0:T(8,128)(2,1)S(1)}, bf16[128,2048]{1,0:T(8,128)(2,1)}, u32[]{:S(2)}, u32[]{:S(2)}) collective-permute-start(bf16[128,2048]{1,0:T(8,128)(2,1)S(1)} %collective-permute-done.2), channel_id=1, source_target_pairs={{2,3},{6,7},{10,11},{14,15}} | collective-permute-start | bytes 1572872 | tf_op jit(solution)/shard_map/ppermute | solution.py:28
  21.8 31.0 %copy-start.5 = (f32[1,3,3,1024]{3,0,2,1:T(1,128)S(1)}, f32[1,3,3,1024]{3,0,2,1:T(1,128)}, u32[]{:S(2)}) copy-start(f32[1,3,3,1024]{3,0,2,1:T(1,128)} %param.11) | copy-start | bytes 110596
  49.7 3.3 collective-permute-start.9
  50.4 2.6 collective-permute-start.8
  51.2 1.9 collective-permute-start.7
  52.0 0.9 collective-permute-start
  117.6 2.9 collective-permute-start.13
  119.3 3.7 collective-permute-start.10
  122.2 3.3 collective-permute-start.14
  124.7 3.3 collective-permute-start.11
  127.2 4.4 collective-permute-start.15
  129.7 1.8 collective-permute-start.12
  133.7 113.6 %collective-permute-start.16 = (bf16[2,192,2048]{2,1,0:T(8,128)(2,1)S(1)}, bf16[2,192,2048]{2,1,0:T(8,128)(2,1)S(1)}, u32[]{:S(2)}, u32[]{:S(2)}) collective-permute-start(bf16[2,192,2048]{2,1,0:T(8,128)(2,1)S(1)} %fusion.29), channel_id=1, source_target_pairs={{0,16},{1,17},{2,18},{3,19},{4,20},{5,21},{6,22},{7,23},{8,24},{9,... | collective-permute-start | bytes 4718600 | tf_op jit(solution)/shard_map/ppermute | solution.py:260
  247.7 20.0 %collective-permute-start.20 = (bf16[384,2048]{1,0:T(8,128)(2,1)S(1)}, bf16[384,2048]{1,0:T(8,128)(2,1)S(1)}, u32[]{:S(2)}, u32[]{:S(2)}) collective-permute-start(bf16[384,2048]{1,0:T(8,128)(2,1)S(1)} %fusion.30), channel_id=1, source_target_pairs={{17,16},{18,17},{19,18},{21,20},{22,21},{23,22},{25,24},{26,25},{2... | collective-permute-start | bytes 4718600 | tf_op jit(solution)/shard_map/ppermute | solution.py:28
  249.3 23.4 %collective-permute-start.17 = (bf16[384,2048]{1,0:T(8,128)(2,1)S(1)}, bf16[384,2048]{1,0:T(8,128)(2,1)S(1)}, u32[]{:S(2)}, u32[]{:S(2)}) collective-permute-start(bf16[384,2048]{1,0:T(8,128)(2,1)S(1)} %fusion.30), channel_id=1, source_target_pairs={{16,17},{17,18},{18,19},{20,21},{21,22},{22,23},{24,25},{25,26},{2... | collective-permute-start | bytes 4718600 | tf_op jit(solution)/shard_map/ppermute | solution.py:28
  268.8 5.2 collective-permute-start.21
  272.7 21.5 %collective-permute-start.18 = (bf16[384,2048]{1,0:T(8,128)(2,1)S(1)}, bf16[384,2048]{1,0:T(8,128)(2,1)}, u32[]{:S(2)}, u32[]{:S(2)}) collective-permute-start(bf16[384,2048]{1,0:T(8,128)(2,1)S(1)} %collective-permute-done.17), channel_id=1, source_target_pairs={{17,18},{18,19},{21,22},{22,23},{25,26},{26,27},{29,30},{30,31}} | collective-permute-start | bytes 4718600 | tf_op jit(solution)/shard_map/ppermute | solution.py:28
  274.0 52.3 %collective-permute-start.22 = (bf16[384,2048]{1,0:T(8,128)(2,1)}, bf16[384,2048]{1,0:T(8,128)(2,1)}, u32[]{:S(2)}, u32[]{:S(2)}) collective-permute-start(bf16[384,2048]{1,0:T(8,128)(2,1)} %collective-permute-done.21), channel_id=1, source_target_pairs={{17,16},{21,20},{25,24},{29,28}} | collective-permute-start | bytes 4718600 | tf_op jit(solution)/shard_map/ppermute | solution.py:28
  294.2 32.1 %collective-permute-start.19 = (bf16[384,2048]{1,0:T(8,128)(2,1)}, bf16[384,2048]{1,0:T(8,128)(2,1)}, u32[]{:S(2)}, u32[]{:S(2)}) collective-permute-start(bf16[384,2048]{1,0:T(8,128)(2,1)} %collective-permute-done.18), channel_id=1, source_target_pairs={{18,19},{22,23},{26,27},{30,31}} | collective-permute-start | bytes 4718600 | tf_op jit(solution)/shard_map/ppermute | solution.py:28
  370.8 7.3 %collective-permute-start.23 = (bf16[2,16,3072]{2,1,0:T(8,128)(2,1)S(1)}, bf16[2,16,3072]{2,1,0:T(8,128)(2,1)S(1)}, u32[]{:S(2)}, u32[]{:S(2)}) collective-permute-start(bf16[2,16,3072]{2,1,0:T(8,128)(2,1)S(1)} %slice.63), channel_id=1, source_target_pairs={{16,20},{20,24},{24,28},{28,16},{17,21},{21,25},{25,29},{29,17},{1... | collective-permute-start | bytes 589832 | tf_op jit(solution)/shard_map/ppermute | solution.py:28
  374.8 10.8 %collective-permute-start.24 = (bf16[2,128,1024]{2,1,0:T(8,128)(2,1)S(1)}, bf16[2,128,1024]{2,1,0:T(8,128)(2,1)S(1)}, u32[]{:S(2)}, u32[]{:S(2)}) collective-permute-start(bf16[2,128,1024]{2,1,0:T(8,128)(2,1)S(1)} %fusion.38), channel_id=1, source_target_pairs={{16,20},{20,24},{24,28},{28,16},{17,21},{21,25},{25,29},{29,17},{1... | collective-permute-start | bytes 1572872 | tf_op jit(solution)/shard_map/ppermute | solution.py:28
  466.1 20.5 %collective-permute-start.28 = (bf16[2,192,2048]{2,1,0:T(8,128)(2,1)S(1)}, bf16[2,192,2048]{2,1,0:T(8,128)(2,1)S(1)}, u32[]{:S(2)}, u32[]{:S(2)}) collective-permute-start(bf16[2,192,2048]{2,1,0:T(8,128)(2,1)S(1)} %bitcast.126), channel_id=1, source_target_pairs={{19,18},{23,22},{27,26},{31,30}} | collective-permute-start | bytes 4718600 | tf_op jit(solution)/shard_map/ppermute | solution.py:28
  470.3 21.9 %collective-permute-start.25 = (bf16[2,192,2048]{2,1,0:T(8,128)(2,1)S(1)}, bf16[2,192,2048]{2,1,0:T(8,128)(2,1)S(1)}, u32[]{:S(2)}, u32[]{:S(2)}) collective-permute-start(bf16[2,192,2048]{2,1,0:T(8,128)(2,1)S(1)} %bitcast.124), channel_id=1, source_target_pairs={{16,17},{20,21},{24,25},{28,29}} | collective-permute-start | bytes 4718600 | tf_op jit(solution)/shard_map/ppermute | solution.py:28
  488.3 21.2 %collective-permute-start.29 = (bf16[2,192,2048]{2,1,0:T(8,128)(2,1)S(1)}, bf16[2,192,2048]{2,1,0:T(8,128)(2,1)S(1)}, u32[]{:S(2)}, u32[]{:S(2)}) collective-permute-start(bf16[2,192,2048]{2,1,0:T(8,128)(2,1)S(1)} %fusion.16), channel_id=1, source_target_pairs={{18,17},{19,18},{22,21},{23,22},{26,25},{27,26},{30,29},{31,30}} | collective-permute-start | bytes 4718600 | tf_op jit(solution)/shard_map/ppermute | solution.py:28
  494.0 22.8 %collective-permute-start.26 = (bf16[2,192,2048]{2,1,0:T(8,128)(2,1)S(1)}, bf16[2,192,2048]{2,1,0:T(8,128)(2,1)S(1)}, u32[]{:S(2)}, u32[]{:S(2)}) collective-permute-start(bf16[2,192,2048]{2,1,0:T(8,128)(2,1)S(1)} %fusion.18), channel_id=1, source_target_pairs={{16,17},{17,18},{20,21},{21,22},{24,25},{25,26},{28,29},{29,30}} | collective-permute-start | bytes 4718600 | tf_op jit(solution)/shard_map/ppermute | solution.py:28
  511.8 21.5 %collective-permute-start.30 = (bf16[2,192,2048]{2,1,0:T(8,128)(2,1)}, bf16[2,192,2048]{2,1,0:T(8,128)(2,1)}, u32[]{:S(2)}, u32[]{:S(2)}) collective-permute-start(bf16[2,192,2048]{2,1,0:T(8,128)(2,1)} %fusion.17), channel_id=1, source_target_pairs={{17,16},{18,17},{19,18},{21,20},{22,21},{23,22},{25,24},{26,25},{2... | collective-permute-start | bytes 4718600 | tf_op jit(solution)/shard_map/ppermute | solution.py:28
  519.1 21.5 %collective-permute-start.27 = (bf16[2,192,2048]{2,1,0:T(8,128)(2,1)}, bf16[2,192,2048]{2,1,0:T(8,128)(2,1)}, u32[]{:S(2)}, u32[]{:S(2)}) collective-permute-start(bf16[2,192,2048]{2,1,0:T(8,128)(2,1)} %fusion.19), channel_id=1, source_target_pairs={{16,17},{17,18},{18,19},{20,21},{21,22},{22,23},{24,25},{25,26},{2... | collective-permute-start | bytes 4718600 | tf_op jit(solution)/shard_map/ppermute | solution.py:28
  (6 other events, 44.5 us)

commit v2 on v1

--- a/solution.py
+++ b/solution.py
@@ -28,36 +28,37 @@
     return lax.ppermute(value, ("pipe", axis), pairs_on(section, axis, links))
 
 
-def gather_features(block, section):
+def arrivals(count):
+    return [
+        [sign * step for step in range(1, count) for sign in (1, -1) if 0 <= at - sign * step < count]
+        for at in range(count)
+    ]
+
+
+def pick(moved, slot):
     count = lax.axis_size("tensor")
-    if count > 4:
-        return lax.all_gather(block, "tensor", axis=0)
     place = lax.axis_index("tensor")
-    up, down = [block], [block]
-    for step in range(1, count):
-        up.append(send_on(up[-1], section, "tensor", [(i, i + 1) for i in range(step - 1, count - 1)]))
-        down.append(send_on(down[-1], section, "tensor", [(i, i - 1) for i in range(1, count - step + 1)]))
-    whole = []
-    for owner in range(count):
-        value = block
-        for step in range(1, count - owner):
-            value = jnp.where(place == owner + step, up[step], value)
-        for step in range(1, owner + 1):
-            value = jnp.where(place == owner - step, down[step], value)
-        whole.append(value)
-    return jnp.stack(whole, axis=0)
+    order = arrivals(count)
+    wanted = [order[at][slot] for at in range(count)]
+    value, owner = moved[wanted[0]], jnp.int32(0) - wanted[0]
+    for at in range(1, count):
+        owner = jnp.where(place == at, at - wanted[at], owner)
+    for hop in sorted(set(wanted) - {wanted[0]}):
+        here = functools.reduce(jnp.logical_or, [place == at for at in range(count) if wanted[at] == hop])
+        value = jnp.where(here, moved[hop], value)
+    return value, owner
 
 
 def scatter_sum(partial, section):
     count = lax.axis_size("tensor")
     place = lax.axis_index("tensor")
     if count > 4:
-        own = lax.psum_scatter(partial, "tensor", scatter_dimension=2, tiled=False)
+        own = lax.psum_scatter(partial, "tensor", scatter_dimension=0, tiled=False)
         return own.astype(jnp.float32)
 
     def block(index):
         index = jnp.clip(index, 0, count - 1)
-        return lax.dynamic_index_in_dim(partial, index, 2, keepdims=False).astype(jnp.float32)
+        return lax.dynamic_index_in_dim(partial, index, 0, keepdims=False).astype(jnp.float32)
 
     up = down = None
     for step in range(1, count):
@@ -76,43 +77,135 @@
     return total
 
 
-def project_kernel(x_ref, w_ref, inv_ref, out_ref, total):
+def project_kernel(has_base, is_last, owner_ref, x_ref, low_ref, high_ref, *refs):
+    refs = list(refs)
+    base_ref = refs.pop(0) if has_base else None
+    inv_ref = refs.pop(0) if is_last else None
+    out_ref, total = refs
     step = pl.program_id(1)
+    half = low_ref.shape[1]
+    rows = total.shape[0]
+    product = jnp.dot(x_ref[:rows, :half], low_ref[0], preferred_element_type=jnp.float32)
+    product += jnp.dot(x_ref[:rows, half:], high_ref[0], preferred_element_type=jnp.float32)
 
     @pl.when(step == 0)
     def _():
-        total[...] = jnp.zeros_like(total)
-
-    total[...] += jnp.dot(x_ref[0], w_ref[0], preferred_element_type=jnp.float32)
+        total[...] = product + base_ref[...] if has_base else product
+
+    @pl.when(step > 0)
+    def _():
+        total[...] += product
 
     @pl.when(step == pl.num_programs(1) - 1)
     def _():
-        out_ref[...] = (total[...] * inv_ref[...]).astype(out_ref.dtype)
-
-
-def project(gathered, weights, inv_rms):
-    count, rows, width = gathered.shape
-    groups, depth, channels = weights.shape
+        result = total[...]
+        if is_last:
+            result = result * inv_ref[...]
+        out_ref[...] = result.astype(out_ref.dtype)
+
+
+def project(chunk, owner, rows, weights, base, inv_rms):
+    length, width = chunk.shape
+    groups, _, channels = weights.shape
+    half = min(width, 1024) // 2
+    steps = width // (2 * half)
+    in_specs = [
+        pl.BlockSpec((length, 2 * half), lambda g, k, o: (0, k)),
+        pl.BlockSpec((1, half, channels), lambda g, k, o: (g, 2 * (o[0] * steps + k), 0)),
+        pl.BlockSpec((1, half, channels), lambda g, k, o: (g, 2 * (o[0] * steps + k) + 1, 0)),
+    ]
+    operands = [chunk, weights, weights]
+    block = pl.BlockSpec((rows, channels), lambda g, k, o: (0, g))
+    if base is not None:
+        in_specs.append(block)
+        operands.append(base)
+    if inv_rms is not None:
+        in_specs.append(pl.BlockSpec((rows, 1), lambda g, k, o: (0, 0)))
+        operands.append(inv_rms)
+    out_type = jnp.float32 if inv_rms is None else jnp.bfloat16
+    return pl.pallas_call(
+        functools.partial(project_kernel, base is not None, inv_rms is not None),
+        grid_spec=pltpu.PrefetchScalarGridSpec(
+            num_scalar_prefetch=1,
+            grid=(groups, steps),
+            in_specs=in_specs,
+            out_specs=block,
+            scratch_shapes=[pltpu.VMEM((rows, channels), jnp.float32)],
+        ),
+        out_shape=jax.ShapeDtypeStruct((rows, groups * channels), out_type),
+        compiler_params=pltpu.CompilerParams(vmem_limit_bytes=VMEM_LIMIT),
+        cost_estimate=pl.CostEstimate(
+            flops=2 * rows * width * groups * channels,
+            bytes_accessed=2 * (groups * width * channels + rows * width),
+            transcendentals=0,
+        ),
+    )(owner.reshape(1).astype(jnp.int32), *operands)
+
+
+def normed_projection(values, gain, weights, section):
+    rows, width = values.shape
+    count = lax.axis_size("tensor")
+    scaled = (values * gain).astype(jnp.bfloat16)
+    squares = jnp.sum(values * values, axis=1)
+    ride = 1 < count <= 4 and rows <= width
+    if ride:
+        parts, rest = [], squares
+        for _ in range(3):
+            part = lax.reduce_precision(rest, 8, 7)
+            parts.append(part.astype(jnp.bfloat16))
+            rest = rest - part
+        packed = jnp.pad(jnp.stack(parts, axis=0), ((0, 13), (0, width - rows)))
+        scaled = jnp.concatenate([scaled, packed], axis=0)
+    if not ride:
+        inv_rms = lax.rsqrt(lax.psum(squares, "tensor") / (width * count) + epsilon)[:, None]
+        gathered = lax.all_gather(scaled, "tensor", axis=1, tiled=True)
+        return project(gathered, jnp.int32(0), rows, weights, None, inv_rms)
+
+    def squares_of(chunk):
+        return jnp.sum(chunk[rows : rows + 3, :rows].astype(jnp.float32), axis=0)
+
+    moved = {0: scaled}
+    chunk, owner = scaled, lax.axis_index("tensor")
+    total, squares = None, squares_of(scaled)
+    for step in range(1, count):
+        up, down = moved[step - 1], moved[1 - step]
+        moved[step] = send_on(up, section, "tensor", [(i, i + 1) for i in range(step - 1, count - 1)])
+        moved[-step] = send_on(down, section, "tensor", [(i, i - 1) for i in range(1, count - step + 1)])
+        total = project(chunk, owner, rows, weights, total, None)
+        moved[step], moved[-step], total = lax.optimization_barrier((moved[step], moved[-step], total))
+        chunk, owner = pick(moved, step - 1)
+        squares = squares + squares_of(chunk)
+    inv_rms = lax.rsqrt(squares / (width * count) + epsilon)[:, None]
+    return project(chunk, owner, rows, weights, total, inv_rms)
+
+
+def out_kernel(y_ref, w_ref, out_ref):
+    product = jnp.dot(y_ref[...], w_ref[...], preferred_element_type=jnp.float32)
+    out_ref[0] = product.astype(out_ref.dtype)
+
+
+def out_product(y_rows, w_down):
+    rows, channels = y_rows.shape
+    count = lax.axis_size("tensor")
+    width = w_down.shape[1] // count
     tile = min(width, 1024)
     per_block = width // tile
     return pl.pallas_call(
-        project_kernel,
-        grid=(groups, depth // tile),
+        out_kernel,
+        grid=(count, per_block),
         in_specs=[
-            pl.BlockSpec((1, rows, tile), lambda g, k: (k // per_block, 0, k % per_block)),
-            pl.BlockSpec((1, tile, channels), lambda g, k: (g, k, 0)),
-            pl.BlockSpec((rows, 1), lambda g, k: (0, 0)),
+            pl.BlockSpec((rows, channels), lambda b, c: (0, 0)),
+            pl.BlockSpec((channels, tile), lambda b, c: (0, b * per_block + c)),
         ],
-        out_specs=pl.BlockSpec((rows, channels), lambda g, k: (0, g)),
-        out_shape=jax.ShapeDtypeStruct((rows, groups * channels), jnp.bfloat16),
-        scratch_shapes=[pltpu.VMEM((rows, channels), jnp.float32)],
+        out_specs=pl.BlockSpec((1, rows, tile), lambda b, c: (b, 0, c)),
+        out_shape=jax.ShapeDtypeStruct((count, rows, width), jnp.bfloat16),
         compiler_params=pltpu.CompilerParams(vmem_limit_bytes=VMEM_LIMIT),
         cost_estimate=pl.CostEstimate(
-            flops=2 * rows * depth * groups * channels,
-            bytes_accessed=2 * (groups * depth * channels + rows * depth),
+            flops=2 * rows * channels * width * count,
+            bytes_accessed=2 * (channels + rows) * width * count,
             transcendentals=0,
         ),
-    )(gathered, weights, inv_rms)
+    )(y_rows, w_down)
 
 
 def mix_kernel(taps_count, has_history, *refs):
@@ -208,19 +301,10 @@
     return jnp.where(shard_pos == 0, earlier, received)
 
 
-def inverse_rms(values):
-    width = values.shape[-1] * lax.axis_size("tensor")
-    squares = lax.psum(jnp.sum(values * values, axis=-1, keepdims=True), "tensor")
-    return lax.rsqrt(squares / width + epsilon)
-
-
 def finish(stream, y_out, w_down, section):
-    count = lax.axis_size("tensor")
-    slices, rows, _ = y_out.shape
-    partial = jnp.einsum("snc,cd->snd", y_out, w_down, preferred_element_type=jnp.float32)
-    partial = partial.astype(jnp.bfloat16).reshape(slices, rows, count, -1)
-    mixed = scatter_sum(partial, section)
-    return (stream.astype(jnp.float32) + mixed).astype(jnp.bfloat16)
+    slices, rows, channels = y_out.shape
+    mixed = scatter_sum(out_product(y_out.reshape(slices * rows, channels), w_down), section)
+    return (stream.astype(jnp.float32) + mixed.reshape(stream.shape)).astype(jnp.bfloat16)
 
 
 def one_hot(ids, vocab):
@@ -239,8 +323,7 @@
 
     share = vocab // shards
     own_rows = lax.dynamic_slice_in_dim(embed_table, shard_pos * share, share, 0).astype(jnp.float32)
-    scaled = gather_features((own_rows * gain).astype(jnp.bfloat16), 0)
-    own_table = project(scaled, weights, inverse_rms(own_rows))
+    own_table = normed_projection(own_rows, gain, weights, 0)
     tables = [own_table]
     for step in range(1, shards):
         tables.append(send_on(own_table, 0, "seq", [(i, i ^ step) for i in range(shards)]))
@@ -259,8 +342,7 @@
 
     stream = lax.ppermute(first, "pipe", [(0, 1)])
     values = stream.reshape(slices * rows, width).astype(jnp.float32)
-    scaled = gather_features((values * gain).astype(jnp.bfloat16), 1)
-    projected = project(scaled, weights, inverse_rms(values)).reshape(slices, rows, -1)
+    projected = normed_projection(values, gain, weights, 1).reshape(slices, rows, -1)
     channels = projected.shape[2] // 3
     tail = projected[:, rows - HEAD :, :]
     late = projected[:, rows - KL - KF + 1 :, channels:].astype(jnp.float32)

time: 552 us -> 438 us (0.79)
  local copies, waits for them, and re-layouts: 93.6 us -> 7.4 us
  blocking collectives: 42.3 us -> 0 us
  Pallas kernels: 89.3 us -> 131 us
  matrix products: 31.6 us -> 5.29 us
  starting transfers between devices: 44.9 us -> 69.3 us
  waiting for transfers between devices: 206 us -> 189 us
  other arithmetic: 38.4 us -> 29.6 us
    dynamic_slice x2 -> x0, local copies, waits for them, and re-layouts: 65.7 us -> none  [block(): lax.dynamic_index_in_dim(partial, index, 2, keepdims=False)]
    psum x2 -> x0, blocking collectives: 42.3 us -> none  [inverse_rms(): lax.psum(jnp.sum(values * values, axis=-1, keepdims=True), 'tensor')]
    pallas_call x2 -> x10, Pallas kernels: 65 us -> 107 us  [the longest x8 79.9 us: project(): pl.pallas_call(functools.partial(project_kernel, base is not None, inv_rm...]
    dot_general x2 -> x0, matrix products: 28.7 us -> none  [finish(): jnp.einsum('snc,cd->snd', y_out, w_down, preferred_element_type=jnp.float32)]
    ppermute x30, starting transfers between devices: 43.6 us -> 68 us  [send_on(): return lax.ppermute(value, ('pipe', axis), pairs_on(section, axis, links))]
    reshape x2 -> x0, local copies, waits for them, and re-layouts: 22.4 us -> none  [finish(): partial = partial.astype(jnp.bfloat16).reshape(slices, rows, count, -1)]
    ppermute x30, waiting for transfers between devices: 93.6 us -> 77.3 us  [send_on(): return lax.ppermute(value, ('pipe', axis), pairs_on(section, axis, links))]
    another operation x4 -> x0, other arithmetic: 8.59 us -> none  [gather_features(): return jnp.stack(whole, axis=0)]
  transfers between devices with their start and end apart: 31 -> 31, of which waited for: 10 -> 9; matrix products, arithmetic and copies ran while one was open for 4% -> 3% of each run, Pallas kernels for 0% -> 14%
where the time goes in v2:
time: 438 us; the launch traced here: 433 us
  waiting for transfers between devices  189 us (43%)
  Pallas kernels  131 us (30%)
  starting transfers between devices  69.3 us (16%)
  other arithmetic  29.6 us (7%)
  local copies, waits for them, and re-layouts  7.4 us (2%)
  matrix products  5.29 us (1%)
    ppermute x1, waiting for transfers between devices, local(): stream = lax.ppermute(first, 'pipe', [(0, 1)])  111 us
    pallas_call x8, Pallas kernels, project(): pl.pallas_call(functools.partial(project_kernel, base is not None, inv_rm...  79.9 us
    ppermute x30, waiting for transfers between devices, send_on(): return lax.ppermute(value, ('pipe', axis), pairs_on(section, axis, links))  77.3 us
    ppermute x30, starting transfers between devices, send_on(): return lax.ppermute(value, ('pipe', axis), pairs_on(section, axis, links))  68 us
    pallas_call x2, Pallas kernels, out_product(): pl.pallas_call(out_kernel, grid=(count, per_block), in_specs=[pl.BlockSpe...  27.2 us
    pallas_call x2, Pallas kernels, mix(): pl.pallas_call(functools.partial(mix_kernel, taps.shape[0], history is no...  24.3 us
    convert_element_type x4, other arithmetic, scatter_sum(): up_block.astype(jnp.bfloat16)  9.32 us
  transfers between devices with their start and end apart: 31, of which 9 were waited for; matrix products, arithmetic and copies ran while one was open for 3% of the time, Pallas kernels for 14%

profile of v2, /device:TPU:25, one launch (start us, length us, event | category | flops | bytes accessed | tf_op | source)
XLA Modules:
  0.0 432.5 jit_solution(7009106129957272603)
XLA Ops:
  3.5 7.5 %shard_map.82.refs_0_ = f32[128,3072]{1,0:T(8,128)S(1)} custom-call(s32[1]{0:T(128)} %bitcast.4.owner_ref, bf16[144,2048]{1,0:T(8,128)(2,1)S(1)} %fusion.28.x_ref, bf16[3,8192,1024]{2,1,0:T(8,128)(2,1)} %bitcast.83, bf16[3,8192,1024]{2,1,0:T(8,128)(2,1)} %bitcast.84), custom_call_target="tpu_custom_call" | custom-call | flops 1610612736 | bytes 13107200 | tf_op jit(solution)/shard_map/pallas_call | solution.py:126
  12.6 7.5 %shard_map.83.refs_0_ = f32[128,3072]{1,0:T(8,128)S(1)} custom-call(s32[1]{0:T(128)} %bitcast.7.owner_ref, bf16[144,2048]{1,0:T(8,128)(2,1)S(1)} %broadcast_select_fusion.1.x_ref, bf16[3,8192,1024]{2,1,0:T(8,128)(2,1)} %bitcast.85, bf16[3,8192,1024]{2,1,0:T(8,128)(2,1)} %bitcast.86, f32[128,3072]{1,0:T(8,128)S(1)} %shard_map.82.refs_0_), custom_call_target="tpu_custom_call" | custom-call | flops 1610612736 | bytes 13107200 | tf_op jit(solution)/shard_map/pallas_call | solution.py:126
  21.7 7.5 %shard_map.84.refs_0_ = f32[128,3072]{1,0:T(8,128)S(1)} custom-call(s32[1]{0:T(128)} %bitcast.9.owner_ref, bf16[144,2048]{1,0:T(8,128)(2,1)S(1)} %select_select_fusion.3.x_ref, bf16[3,8192,1024]{2,1,0:T(8,128)(2,1)} %bitcast.87, bf16[3,8192,1024]{2,1,0:T(8,128)(2,1)} %bitcast.88, f32[128,3072]{1,0:T(8,128)S(1)} %shard_map.83.refs_0_), custom_call_target="tpu_custom_call" | custom-call | flops 1610612736 | bytes 13107200 | tf_op jit(solution)/shard_map/pallas_call | solution.py:126
  29.5 7.7 %shard_map.85 = bf16[128,3072]{1,0:T(8,128)(2,1)S(1)} custom-call(s32[1]{0:T(128)} %bitcast.1.owner_ref, bf16[144,2048]{1,0:T(8,128)(2,1)S(1)} %select_select_fusion.2.x_ref, bf16[3,8192,1024]{2,1,0:T(8,128)(2,1)} %bitcast.89, bf16[3,8192,1024]{2,1,0:T(8,128)(2,1)} %bitcast.90, f32[128,3072]{1,0:T(8,128)S(1)} %shard_map.84.refs_0_, f32[128,1]{1,0:T(8,128)S(1)} %copy.10.refs_1_), custom_call_target="tpu_custom_call" | custom-call | flops 1610612736 | bytes 13107200 | tf_op jit(solution)/shard_map/pallas_call | solution.py:126
  41.1 2.7 convolution_convert_fusion.refs_0_.refs_1_.refs_2_
  43.9 3.7 shard_map.86
  47.6 13.6 %shard_map.87 = bf16[4,384,2048]{2,1,0:T(8,128)(2,1)} custom-call(bf16[384,1024]{1,0:T(8,128)(2,1)S(1)} %bitcast.80, bf16[1024,8192]{1,0:T(8,128)(2,1)} %bitcast.99), custom_call_target="tpu_custom_call" | custom-call | flops 6442450944 | bytes 23068672 | tf_op jit(solution)/shard_map/pallas_call | solution.py:193
  61.1 3.3 dynamic-slice_bitcast_fusion.3
  71.4 4.8 %fusion.15 = (bf16[384,2048]{1,0:T(8,128)(2,1)S(1)}, bf16[384,2048]{1,0:T(8,128)(2,1)}) fusion(bf16[384,2048]{1,0:T(8,128)(2,1)} %collective-permute-done.11, bf16[4,384,2048]{2,1,0:T(8,128)(2,1)} %shard_map.87, s32[]{:T(128)S(6)} %min.30, bf16[384,2048]{1,0:T(8,128)(2,1)S(1)} %collective-permute-done.13, s32[]{:T(128)S(6)} %min.34), kind=kLoop, calls=%fused_computation.27 | loop fusion | flops 6291456 | bytes 9437192 | tf_op jit(solution)/shard_map/convert_element_type | solution.py:70
  78.8 3.2 fusion.13
  85.5 2.7 fusion.16
  90.0 111.4 %collective-permute-done.16 = bf16[2,192,2048]{2,1,0:T(8,128)(2,1)S(1)} collective-permute-done((bf16[2,192,2048]{2,1,0:T(8,128)(2,1)S(1)}, bf16[2,192,2048]{2,1,0:T(8,128)(2,1)S(1)}, u32[]{:S(2)}, u32[]{:S(2)}) %collective-permute-start.16) | collective-permute-done | bytes 1572896 | tf_op jit(solution)/shard_map/ppermute | solution.py:343
  202.8 4.1 collective-permute-start.18
  208.2 11.9 %shard_map.88.refs_0_ = f32[384,3072]{1,0:T(8,128)} custom-call(s32[1]{0:T(128)} %bitcast.4.owner_ref, bf16[400,2048]{1,0:T(8,128)(2,1)S(1)} %fusion.21.x_ref, bf16[3,8192,1024]{2,1,0:T(8,128)(2,1)} %bitcast.91, bf16[3,8192,1024]{2,1,0:T(8,128)(2,1)} %bitcast.92), custom_call_target="tpu_custom_call" | custom-call | flops 4831838208 | bytes 14155776 | tf_op jit(solution)/shard_map/pallas_call | solution.py:126
  220.1 4.7 %collective-permute-done.18 = bf16[400,2048]{1,0:T(8,128)(2,1)S(1)} collective-permute-done((bf16[400,2048]{1,0:T(8,128)(2,1)S(1)}, bf16[400,2048]{1,0:T(8,128)(2,1)S(1)}, u32[]{:S(2)}, u32[]{:S(2)}) %collective-permute-start.18) | collective-permute-done | bytes 1638432 | tf_op jit(solution)/shard_map/ppermute | solution.py:28
  224.8 4.1 collective-permute-done.17
  231.2 12.8 %shard_map.89.refs_0_ = f32[384,3072]{1,0:T(8,128)} custom-call(s32[1]{0:T(128)} %bitcast.7.owner_ref, bf16[400,2048]{1,0:T(8,128)(2,1)S(1)} %broadcast_select_fusion.x_ref, bf16[3,8192,1024]{2,1,0:T(8,128)(2,1)} %bitcast.93, bf16[3,8192,1024]{2,1,0:T(8,128)(2,1)} %bitcast.94, f32[384,3072]{1,0:T(8,128)} %shard_map.88.refs_0_), custom_call_target="tpu_custom_call" | custom-call | flops 4831838208 | bytes 14155776 | tf_op jit(solution)/shard_map/pallas_call | solution.py:126
  243.9 6.9 %collective-permute-done.19 = bf16[400,2048]{1,0:T(8,128)(2,1)S(1)} collective-permute-done((bf16[400,2048]{1,0:T(8,128)(2,1)S(1)}, bf16[400,2048]{1,0:T(8,128)(2,1)S(1)}, u32[]{:S(2)}, u32[]{:S(2)}) %collective-permute-start.19) | collective-permute-done | bytes 1638432 | tf_op jit(solution)/shard_map/ppermute | solution.py:28
  253.1 12.8 %shard_map.90.refs_0_ = f32[384,3072]{1,0:T(8,128)} custom-call(s32[1]{0:T(128)} %bitcast.9.owner_ref, bf16[400,2048]{1,0:T(8,128)(2,1)S(1)} %select_select_fusion.1.x_ref, bf16[3,8192,1024]{2,1,0:T(8,128)(2,1)} %bitcast.95, bf16[3,8192,1024]{2,1,0:T(8,128)(2,1)} %bitcast.96, f32[384,3072]{1,0:T(8,128)} %shard_map.89.refs_0_), custom_call_target="tpu_custom_call" | custom-call | flops 4831838208 | bytes 14155776 | tf_op jit(solution)/shard_map/pallas_call | solution.py:126
  265.9 7.7 %collective-permute-done.21 = bf16[400,2048]{1,0:T(8,128)(2,1)S(1)} collective-permute-done((bf16[400,2048]{1,0:T(8,128)(2,1)S(1)}, bf16[400,2048]{1,0:T(8,128)(2,1)S(1)}, u32[]{:S(2)}, u32[]{:S(2)}) %collective-permute-start.21) | collective-permute-done | bytes 1638432 | tf_op jit(solution)/shard_map/ppermute | solution.py:28
  274.0 12.2 %shard_map.91 = bf16[384,3072]{1,0:T(8,128)(2,1)} custom-call(s32[1]{0:T(128)} %bitcast.1.owner_ref, bf16[400,2048]{1,0:T(8,128)(2,1)S(1)} %select_select_fusion.x_ref, bf16[3,8192,1024]{2,1,0:T(8,128)(2,1)} %bitcast.97, bf16[3,8192,1024]{2,1,0:T(8,128)(2,1)} %bitcast.98, f32[384,3072]{1,0:T(8,128)} %shard_map.90.refs_0_, f32[384,1]{1,0:T(8,128)S(1)} %reshape.375.refs_1_), custom_call_target="tpu_custom_call" | custom-call | flops 4831838208 | bytes 14155776 | tf_op jit(solution)/shard_map/pallas_call | solution.py:126
  288.7 3.3 collective-permute-start.23
  292.8 3.3 collective-permute-start.24
  297.8 5.9 %collective-permute-done.24 = bf16[2,128,1024]{2,1,0:T(8,128)(2,1)S(1)} collective-permute-done((bf16[2,128,1024]{2,1,0:T(8,128)(2,1)S(1)}, bf16[2,128,1024]{2,1,0:T(8,128)(2,1)S(1)}, u32[]{:S(2)}, u32[]{:S(2)}) %collective-permute-start.24) | collective-permute-done | bytes 524320 | tf_op jit(solution)/shard_map/ppermute | solution.py:28
  303.8 20.6 %shard_map.92 = bf16[2,192,1024]{2,1,0:T(8,128)(2,1)S(1)} custom-call(bf16[2,208,3072]{2,1,0:T(8,128)(2,1)} %pad_maximum_fusion.refs_0_.refs_1_.refs_2_, bf16[2,208,3072]{2,1,0:T(8,128)(2,1)} %pad_maximum_fusion.refs_0_.refs_1_.refs_2_, bf16[2,208,3072]{2,1,0:T(8,128)(2,1)} %pad_maximum_fusion.refs_0_.refs_1_.refs_2_, ...), custom_call_target="tpu_custom_call" | custom-call | flops 100663296 | bytes 3407872 | tf_op jit(solution)/shard_map/pallas_call | solution.py:279
  324.5 13.6 %shard_map.93 = bf16[4,384,2048]{2,1,0:T(8,128)(2,1)} custom-call(bf16[384,1024]{1,0:T(8,128)(2,1)S(1)} %bitcast.79, bf16[1024,8192]{1,0:T(8,128)(2,1)} %bitcast.100), custom_call_target="tpu_custom_call" | custom-call | flops 6442450944 | bytes 23068672 | tf_op jit(solution)/shard_map/pallas_call | solution.py:193
  344.3 15.8 %collective-permute-done.28 = bf16[384,2048]{1,0:T(8,128)(2,1)S(1)} collective-permute-done((bf16[384,2048]{1,0:T(8,128)(2,1)S(1)}, bf16[384,2048]{1,0:T(8,128)(2,1)S(1)}, u32[]{:S(2)}, u32[]{:S(2)}) %collective-permute-start.28) | collective-permute-done | bytes 1572896 | tf_op jit(solution)/shard_map/ppermute | solution.py:28
  361.6 26.8 %collective-permute-start.29 = (bf16[384,2048]{1,0:T(8,128)(2,1)S(1)}, bf16[384,2048]{1,0:T(8,128)(2,1)S(1)}, u32[]{:S(2)}, u32[]{:S(2)}) collective-permute-start(bf16[384,2048]{1,0:T(8,128)(2,1)S(1)} %get-tuple-element.46), channel_id=1, source_target_pairs={{18,17},{19,18},{22,21},{23,22},{26,25},{27,26},{30,29},{31,30}} | collective-permute-start | bytes 4718600 | tf_op jit(solution)/shard_map/ppermute | solution.py:28
  389.7 15.9 %collective-permute-done.29 = bf16[384,2048]{1,0:T(8,128)(2,1)S(1)} collective-permute-done((bf16[384,2048]{1,0:T(8,128)(2,1)S(1)}, bf16[384,2048]{1,0:T(8,128)(2,1)S(1)}, u32[]{:S(2)}, u32[]{:S(2)}) %collective-permute-start.29) | collective-permute-done | bytes 1572896 | tf_op jit(solution)/shard_map/ppermute | solution.py:28
  406.2 5.0 %collective-permute-start.30 = (bf16[384,2048]{1,0:T(8,128)(2,1)S(1)}, bf16[384,2048]{1,0:T(8,128)(2,1)}, u32[]{:S(2)}, u32[]{:S(2)}) collective-permute-start(bf16[384,2048]{1,0:T(8,128)(2,1)S(1)} %fusion.8), channel_id=1, source_target_pairs={{17,16},{18,17},{19,18},{21,20},{22,21},{23,22},{25,24},{26,25},{2... | collective-permute-start | bytes 4718600 | tf_op jit(solution)/shard_map/ppermute | solution.py:28
  411.2 16.2 %collective-permute-done.30 = bf16[384,2048]{1,0:T(8,128)(2,1)} collective-permute-done((bf16[384,2048]{1,0:T(8,128)(2,1)S(1)}, bf16[384,2048]{1,0:T(8,128)(2,1)}, u32[]{:S(2)}, u32[]{:S(2)}) %collective-permute-start.30) | collective-permute-done | bytes 1572896 | tf_op jit(solution)/shard_map/ppermute | solution.py:28
  427.4 3.2 fusion.11
  (122 shorter events, 49.4 us)
Async XLA Ops:
  2.1 9.0 %collective-permute-start.2 = (bf16[144,2048]{1,0:T(8,128)(2,1)S(1)}, bf16[144,2048]{1,0:T(8,128)(2,1)S(1)}, u32[]{:S(2)}, u32[]{:S(2)}) collective-permute-start(bf16[144,2048]{1,0:T(8,128)(2,1)S(1)} %fusion.28.x_ref), channel_id=1, source_target_pairs={{1,0},{2,1},{3,2},{5,4},{6,5},{7,6},{9,8},{10,9},{11,10},{13,12},{... | collective-permute-start | bytes 1769480 | tf_op jit(solution)/shard_map/ppermute | solution.py:28
  2.8 8.3 %collective-permute-start.1 = (bf16[144,2048]{1,0:T(8,128)(2,1)S(1)}, bf16[144,2048]{1,0:T(8,128)(2,1)S(1)}, u32[]{:S(2)}, u32[]{:S(2)}) collective-permute-start(bf16[144,2048]{1,0:T(8,128)(2,1)S(1)} %fusion.28.x_ref), channel_id=1, source_target_pairs={{0,1},{1,2},{2,3},{4,5},{5,6},{6,7},{8,9},{9,10},{10,11},{12,13},{... | collective-permute-start | bytes 1769480 | tf_op jit(solution)/shard_map/ppermute | solution.py:28
  11.1 9.1 %collective-permute-start.3 = (bf16[144,2048]{1,0:T(8,128)(2,1)S(1)}, bf16[144,2048]{1,0:T(8,128)(2,1)S(1)}, u32[]{:S(2)}, u32[]{:S(2)}) collective-permute-start(bf16[144,2048]{1,0:T(8,128)(2,1)S(1)} %collective-permute-done.1), channel_id=1, source_target_pairs={{1,2},{2,3},{5,6},{6,7},{9,10},{10,11},{13,14},{14,15}} | collective-permute-start | bytes 1769480 | tf_op jit(solution)/shard_map/ppermute | solution.py:28
  11.8 8.4 %collective-permute-start.4 = (bf16[144,2048]{1,0:T(8,128)(2,1)S(1)}, bf16[144,2048]{1,0:T(8,128)(2,1)S(1)}, u32[]{:S(2)}, u32[]{:S(2)}) collective-permute-start(bf16[144,2048]{1,0:T(8,128)(2,1)S(1)} %collective-permute-done.2), channel_id=1, source_target_pairs={{1,0},{2,1},{5,4},{6,5},{9,8},{10,9},{13,12},{14,13}} | collective-permute-start | bytes 1769480 | tf_op jit(solution)/shard_map/ppermute | solution.py:28
  20.2 9.1 %collective-permute-start.5 = (bf16[144,2048]{1,0:T(8,128)(2,1)S(1)}, bf16[144,2048]{1,0:T(8,128)(2,1)S(1)}, u32[]{:S(2)}, u32[]{:S(2)}) collective-permute-start(bf16[144,2048]{1,0:T(8,128)(2,1)S(1)} %collective-permute-done.3), channel_id=1, source_target_pairs={{2,3},{6,7},{10,11},{14,15}} | collective-permute-start | bytes 1769480 | tf_op jit(solution)/shard_map/ppermute | solution.py:28
  20.9 8.4 %collective-permute-start.6 = (bf16[144,2048]{1,0:T(8,128)(2,1)S(1)}, bf16[144,2048]{1,0:T(8,128)(2,1)S(1)}, u32[]{:S(2)}, u32[]{:S(2)}) collective-permute-start(bf16[144,2048]{1,0:T(8,128)(2,1)S(1)} %collective-permute-done.4), channel_id=1, source_target_pairs={{1,0},{5,4},{9,8},{13,12}} | collective-permute-start | bytes 1769480 | tf_op jit(solution)/shard_map/ppermute | solution.py:28
  37.2 3.9 collective-permute-start.9
  37.9 3.2 collective-permute-start.8
  38.6 2.5 collective-permute-start.7
  40.3 0.7 collective-permute-start
  64.5 2.6 collective-permute-start.10
  66.3 5.1 %collective-permute-start.13 = (bf16[384,2048]{1,0:T(8,128)(2,1)}, bf16[384,2048]{1,0:T(8,128)(2,1)S(1)}, u32[]{:S(2)}, u32[]{:S(2)}) collective-permute-start(bf16[384,2048]{1,0:T(8,128)(2,1)} %get-tuple-element.52), channel_id=1, source_target_pairs={{3,2},{7,6},{11,10},{15,14}} | collective-permute-start | bytes 4718600 | tf_op jit(solution)/shard_map/ppermute | solution.py:28
  69.6 1.8 collective-permute-start.11
  76.2 2.6 collective-permute-start.14
  77.0 8.5 %collective-permute-start.12 = (bf16[384,2048]{1,0:T(8,128)(2,1)S(1)}, bf16[384,2048]{1,0:T(8,128)(2,1)}, u32[]{:S(2)}, u32[]{:S(2)}) collective-permute-start(bf16[384,2048]{1,0:T(8,128)(2,1)S(1)} %get-tuple-element.49), channel_id=1, source_target_pairs={{0,1},{1,2},{2,3},{4,5},{5,6},{6,7},{8,9},{9,10},{10,11},{12,13},{... | collective-permute-start | bytes 4718600 | tf_op jit(solution)/shard_map/ppermute | solution.py:28
  81.9 3.6 collective-permute-start.15
  88.7 112.7 %copy-start.8 = (bf16[2,192,2048]{2,1,0:T(8,128)(2,1)}, bf16[2,192,2048]{2,1,0:T(8,128)(2,1)S(1)}, u32[]{:S(2)}) copy-start(bf16[2,192,2048]{2,1,0:T(8,128)(2,1)S(1)} %add_convert_fusion.1) | copy-start | bytes 4718596
  88.7 112.7 %collective-permute-start.16 = (bf16[2,192,2048]{2,1,0:T(8,128)(2,1)S(1)}, bf16[2,192,2048]{2,1,0:T(8,128)(2,1)S(1)}, u32[]{:S(2)}, u32[]{:S(2)}) collective-permute-start(bf16[2,192,2048]{2,1,0:T(8,128)(2,1)S(1)} %add_convert_fusion.1), channel_id=1, source_target_pairs={{0,16},{1,17},{2,18},{3,19},{4,20},{5,21},{6,22},{7,23},{8,24},{9,... | collective-permute-start | bytes 4718600 | tf_op jit(solution)/shard_map/ppermute | solution.py:343
  202.8 22.1 %collective-permute-start.18 = (bf16[400,2048]{1,0:T(8,128)(2,1)S(1)}, bf16[400,2048]{1,0:T(8,128)(2,1)S(1)}, u32[]{:S(2)}, u32[]{:S(2)}) collective-permute-start(bf16[400,2048]{1,0:T(8,128)(2,1)S(1)} %fusion.21.x_ref), channel_id=1, source_target_pairs={{17,16},{18,17},{19,18},{21,20},{22,21},{23,22},{25,24},{26,25},{2... | collective-permute-start | bytes 4915208 | tf_op jit(solution)/shard_map/ppermute | solution.py:28
  206.9 22.0 %collective-permute-start.17 = (bf16[400,2048]{1,0:T(8,128)(2,1)S(1)}, bf16[400,2048]{1,0:T(8,128)(2,1)S(1)}, u32[]{:S(2)}, u32[]{:S(2)}) collective-permute-start(bf16[400,2048]{1,0:T(8,128)(2,1)S(1)} %fusion.21.x_ref), channel_id=1, source_target_pairs={{16,17},{17,18},{18,19},{20,21},{21,22},{22,23},{24,25},{25,26},{2... | collective-permute-start | bytes 4915208 | tf_op jit(solution)/shard_map/ppermute | solution.py:28
  228.9 21.9 %collective-permute-start.19 = (bf16[400,2048]{1,0:T(8,128)(2,1)S(1)}, bf16[400,2048]{1,0:T(8,128)(2,1)S(1)}, u32[]{:S(2)}, u32[]{:S(2)}) collective-permute-start(bf16[400,2048]{1,0:T(8,128)(2,1)S(1)} %collective-permute-done.17), channel_id=1, source_target_pairs={{17,18},{18,19},{21,22},{22,23},{25,26},{26,27},{29,30},{30,31}} | collective-permute-start | bytes 4915208 | tf_op jit(solution)/shard_map/ppermute | solution.py:28
  230.2 20.6 %collective-permute-start.20 = (bf16[400,2048]{1,0:T(8,128)(2,1)S(1)}, bf16[400,2048]{1,0:T(8,128)(2,1)S(1)}, u32[]{:S(2)}, u32[]{:S(2)}) collective-permute-start(bf16[400,2048]{1,0:T(8,128)(2,1)S(1)} %collective-permute-done.18), channel_id=1, source_target_pairs={{17,16},{18,17},{21,20},{22,21},{25,24},{26,25},{29,28},{30,29}} | collective-permute-start | bytes 4915208 | tf_op jit(solution)/shard_map/ppermute | solution.py:28
  250.8 22.8 %collective-permute-start.21 = (bf16[400,2048]{1,0:T(8,128)(2,1)S(1)}, bf16[400,2048]{1,0:T(8,128)(2,1)S(1)}, u32[]{:S(2)}, u32[]{:S(2)}) collective-permute-start(bf16[400,2048]{1,0:T(8,128)(2,1)S(1)} %collective-permute-done.19), channel_id=1, source_target_pairs={{18,19},{22,23},{26,27},{30,31}} | collective-permute-start | bytes 4915208 | tf_op jit(solution)/shard_map/ppermute | solution.py:28
  252.1 21.5 %collective-permute-start.22 = (bf16[400,2048]{1,0:T(8,128)(2,1)S(1)}, bf16[400,2048]{1,0:T(8,128)(2,1)S(1)}, u32[]{:S(2)}, u32[]{:S(2)}) collective-permute-start(bf16[400,2048]{1,0:T(8,128)(2,1)S(1)} %collective-permute-done.20), channel_id=1, source_target_pairs={{17,16},{21,20},{25,24},{29,28}} | collective-permute-start | bytes 4915208 | tf_op jit(solution)/shard_map/ppermute | solution.py:28
  288.7 7.4 %collective-permute-start.23 = (bf16[2,16,3072]{2,1,0:T(8,128)(2,1)S(1)}, bf16[2,16,3072]{2,1,0:T(8,128)(2,1)S(1)}, u32[]{:S(2)}, u32[]{:S(2)}) collective-permute-start(bf16[2,16,3072]{2,1,0:T(8,128)(2,1)S(1)} %slice.95), channel_id=1, source_target_pairs={{16,20},{20,24},{24,28},{28,16},{17,21},{21,25},{25,29},{29,17},{1... | collective-permute-start | bytes 589832 | tf_op jit(solution)/shard_map/ppermute | solution.py:28
  292.8 11.0 %collective-permute-start.24 = (bf16[2,128,1024]{2,1,0:T(8,128)(2,1)S(1)}, bf16[2,128,1024]{2,1,0:T(8,128)(2,1)S(1)}, u32[]{:S(2)}, u32[]{:S(2)}) collective-permute-start(bf16[2,128,1024]{2,1,0:T(8,128)(2,1)S(1)} %fusion.27), channel_id=1, source_target_pairs={{16,20},{20,24},{24,28},{28,16},{17,21},{21,25},{25,29},{29,17},{1... | collective-permute-start | bytes 1572872 | tf_op jit(solution)/shard_map/ppermute | solution.py:28
  340.5 2.5 collective-permute-start.25
  341.4 18.8 %collective-permute-start.28 = (bf16[384,2048]{1,0:T(8,128)(2,1)S(1)}, bf16[384,2048]{1,0:T(8,128)(2,1)S(1)}, u32[]{:S(2)}, u32[]{:S(2)}) collective-permute-start(bf16[384,2048]{1,0:T(8,128)(2,1)S(1)} %get-tuple-element.48), channel_id=1, source_target_pairs={{19,18},{23,22},{27,26},{31,30}} | collective-permute-start | bytes 4718600 | tf_op jit(solution)/shard_map/ppermute | solution.py:28
  343.6 16.6 %collective-permute-start.26 = (bf16[384,2048]{1,0:T(8,128)(2,1)S(1)}, bf16[384,2048]{1,0:T(8,128)(2,1)S(1)}, u32[]{:S(2)}, u32[]{:S(2)}) collective-permute-start(bf16[384,2048]{1,0:T(8,128)(2,1)S(1)} %fusion.9), channel_id=1, source_target_pairs={{16,17},{17,18},{20,21},{21,22},{24,25},{25,26},{28,29},{29,30}} | collective-permute-start | bytes 4718600 | tf_op jit(solution)/shard_map/ppermute | solution.py:28
  361.6 44.0 %collective-permute-start.29 = (bf16[384,2048]{1,0:T(8,128)(2,1)S(1)}, bf16[384,2048]{1,0:T(8,128)(2,1)S(1)}, u32[]{:S(2)}, u32[]{:S(2)}) collective-permute-start(bf16[384,2048]{1,0:T(8,128)(2,1)S(1)} %get-tuple-element.46), channel_id=1, source_target_pairs={{18,17},{19,18},{22,21},{23,22},{26,25},{27,26},{30,29},{31,30}} | collective-permute-start | bytes 4718600 | tf_op jit(solution)/shard_map/ppermute | solution.py:28
  388.4 22.8 %collective-permute-start.27 = (bf16[384,2048]{1,0:T(8,128)(2,1)S(1)}, bf16[384,2048]{1,0:T(8,128)(2,1)}, u32[]{:S(2)}, u32[]{:S(2)}) collective-permute-start(bf16[384,2048]{1,0:T(8,128)(2,1)S(1)} %get-tuple-element.45), channel_id=1, source_target_pairs={{16,17},{17,18},{18,19},{20,21},{21,22},{22,23},{24,25},{25,26},{2... | collective-permute-start | bytes 4718600 | tf_op jit(solution)/shard_map/ppermute | solution.py:28
  406.2 21.2 %collective-permute-start.30 = (bf16[384,2048]{1,0:T(8,128)(2,1)S(1)}, bf16[384,2048]{1,0:T(8,128)(2,1)}, u32[]{:S(2)}, u32[]{:S(2)}) collective-permute-start(bf16[384,2048]{1,0:T(8,128)(2,1)S(1)} %fusion.8), channel_id=1, source_target_pairs={{17,16},{18,17},{19,18},{21,20},{22,21},{23,22},{25,24},{26,25},{2... | collective-permute-start | bytes 4718600 | tf_op jit(solution)/shard_map/ppermute | solution.py:28
  (11 other events, 89.7 us)

commit v3 on v2

--- a/solution.py
+++ b/solution.py
@@ -179,8 +179,10 @@
     return project(chunk, owner, rows, weights, total, inv_rms)
 
 
-def out_kernel(y_ref, w_ref, out_ref):
-    product = jnp.dot(y_ref[...], w_ref[...], preferred_element_type=jnp.float32)
+def out_kernel(y_ref, low_ref, high_ref, out_ref):
+    half = low_ref.shape[0]
+    product = jnp.dot(y_ref[:, :half], low_ref[...], preferred_element_type=jnp.float32)
+    product += jnp.dot(y_ref[:, half:], high_ref[...], preferred_element_type=jnp.float32)
     out_ref[0] = product.astype(out_ref.dtype)
 
 
@@ -195,7 +197,8 @@
         grid=(count, per_block),
         in_specs=[
             pl.BlockSpec((rows, channels), lambda b, c: (0, 0)),
-            pl.BlockSpec((channels, tile), lambda b, c: (0, b * per_block + c)),
+            pl.BlockSpec((channels // 2, tile), lambda b, c: (0, b * per_block + c)),
+            pl.BlockSpec((channels // 2, tile), lambda b, c: (1, b * per_block + c)),
         ],
         out_specs=pl.BlockSpec((1, rows, tile), lambda b, c: (b, 0, c)),
         out_shape=jax.ShapeDtypeStruct((count, rows, width), jnp.bfloat16),
@@ -205,7 +208,7 @@
             bytes_accessed=2 * (channels + rows) * width * count,
             transcendentals=0,
         ),
-    )(y_rows, w_down)
+    )(y_rows, w_down, w_down)
 
 
 def mix_kernel(taps_count, has_history, *refs):
@@ -259,29 +262,29 @@
     out_ref[0] = (featured(q_ref, 0, 0) * total).astype(out_ref.dtype)
 
 
-def mix(extended, history, feat_taps, taps):
-    slices, length, wide_channels = extended.shape
+def mix(extended, history, feat_taps, taps, part):
+    _, length, wide_channels = extended.shape
     channels = wide_channels // 3
     rows = length - HEAD
     lanes = 128
     blocks = channels // lanes
     in_specs = [
-        pl.BlockSpec((1, length, lanes), functools.partial(lambda g, s, c: (s, 0, g * blocks + c), g))
+        pl.BlockSpec((1, length, lanes), functools.partial(lambda g, c: (part, 0, g * blocks + c), g))
         for g in range(3)
     ]
     operands = [extended, extended, extended]
     if history is not None:
-        in_specs.append(pl.BlockSpec((1, KL, lanes), lambda s, c: (s, 0, c)))
+        in_specs.append(pl.BlockSpec((1, KL, lanes), lambda c: (part, 0, c)))
         operands.append(history)
-    in_specs.append(pl.BlockSpec((KF, 3, lanes), lambda s, c: (0, 0, c)))
-    in_specs.append(pl.BlockSpec((taps.shape[0], lanes), lambda s, c: (0, c)))
+    in_specs.append(pl.BlockSpec((KF, 3, lanes), lambda c: (0, 0, c)))
+    in_specs.append(pl.BlockSpec((taps.shape[0], lanes), lambda c: (0, c)))
     operands += [feat_taps, taps]
     return pl.pallas_call(
         functools.partial(mix_kernel, taps.shape[0], history is not None),
-        grid=(slices, blocks),
+        grid=(blocks,),
         in_specs=in_specs,
-        out_specs=pl.BlockSpec((1, rows, lanes), lambda s, c: (s, 0, c)),
-        out_shape=jax.ShapeDtypeStruct((slices, rows, channels), jnp.bfloat16),
+        out_specs=pl.BlockSpec((1, rows, lanes), lambda c: (0, 0, c)),
+        out_shape=jax.ShapeDtypeStruct((1, rows, channels), jnp.bfloat16),
         scratch_shapes=[
             pltpu.VMEM((length, lanes), jnp.float32),
             pltpu.VMEM((KL + rows, lanes), jnp.float32),
@@ -289,8 +292,8 @@
         ],
         compiler_params=pltpu.CompilerParams(vmem_limit_bytes=VMEM_LIMIT),
         cost_estimate=pl.CostEstimate(
-            flops=2 * taps.shape[0] * slices * rows * channels,
-            bytes_accessed=2 * slices * length * 4 * channels,
+            flops=2 * taps.shape[0] * rows * channels,
+            bytes_accessed=2 * length * 4 * channels,
             transcendentals=0,
         ),
     )(*operands)
@@ -302,9 +305,8 @@
 
 
 def finish(stream, y_out, w_down, section):
-    slices, rows, channels = y_out.shape
-    mixed = scatter_sum(out_product(y_out.reshape(slices * rows, channels), w_down), section)
-    return (stream.astype(jnp.float32) + mixed.reshape(stream.shape)).astype(jnp.bfloat16)
+    mixed = scatter_sum(out_product(y_out[0], w_down), section)
+    return (stream.astype(jnp.float32) + mixed).astype(jnp.bfloat16)
 
 
 def one_hot(ids, vocab):
@@ -337,11 +339,13 @@
     embedded = jnp.einsum(
         "snv,vd->snd", one_hot(token_ids, vocab), embed_table, preferred_element_type=jnp.float32
     ).astype(jnp.bfloat16)
-    y_out = mix(extended, None, feat_taps[0], se_taps)
-    first = finish(embedded, y_out, out_proj[0], 0)
-
-    stream = lax.ppermute(first, "pipe", [(0, 1)])
-    values = stream.reshape(slices * rows, width).astype(jnp.float32)
+    firsts = []
+    for part in range(slices):
+        y_out = mix(extended, None, feat_taps[0], se_taps, part)
+        firsts.append(finish(embedded[part], y_out, out_proj[0], 0))
+
+    streams = [lax.ppermute(first, "pipe", [(0, 1)]) for first in firsts]
+    values = jnp.concatenate(streams, axis=0).astype(jnp.float32)
     projected = normed_projection(values, gain, weights, 1).reshape(slices, rows, -1)
     channels = projected.shape[2] // 3
     tail = projected[:, rows - HEAD :, :]
@@ -352,9 +356,12 @@
     history = after_previous(send_on(gated_tail, 1, "seq", ring), shard_pos, 0)
     head = after_previous(send_on(tail, 1, "seq", ring), shard_pos, 0)
     extended = jnp.concatenate([head, projected], axis=1)
-    y_out = mix(extended, history, feat_taps[0], mr_taps)
-    second = finish(stream, y_out, out_proj[0], 1)
-    return jnp.where(section == 0, first, second)[None]
+    outputs = []
+    for part in range(slices):
+        y_out = mix(extended, history, feat_taps[0], mr_taps, part)
+        second = finish(streams[part], y_out, out_proj[0], 1)
+        outputs.append(jnp.where(section == 0, firsts[part], second))
+    return jnp.stack(outputs, axis=0)[None]
 
 
 def solution(mesh):

time: 438 us -> 407 us (0.929)
  waiting for transfers between devices: 189 us -> 46.1 us
  starting transfers between devices: 69.3 us -> 161 us
  Pallas kernels: 131 us -> 143 us
  other arithmetic: 29.6 us -> 37.9 us
    ppermute x1 -> x2, waiting for transfers between devices: 111 us -> 2.76 us  [local(): streams = [lax.ppermute(first, 'pipe', [(0, 1)]) for first in firsts]]
    ppermute x1 -> x2, starting transfers between devices: 1.29 us -> 76.4 us  [local(): streams = [lax.ppermute(first, 'pipe', [(0, 1)]) for first in firsts]]
    ppermute x30 -> x42, waiting for transfers between devices: 77.3 us -> 43.4 us  [send_on(): return lax.ppermute(value, ('pipe', axis), pairs_on(section, axis, links))]
    ppermute x30 -> x42, starting transfers between devices: 68 us -> 84.6 us  [send_on(): return lax.ppermute(value, ('pipe', axis), pairs_on(section, axis, links))]
    pallas_call x2 -> x4, Pallas kernels: 27.2 us -> 39.3 us  [out_product(): pl.pallas_call(out_kernel, grid=(count, per_block), in_specs=[pl.BlockSpe...]
    add x2 -> x0, other arithmetic: 5.85 us -> none  [scatter_sum(): total = total + up.astype(jnp.float32) + down.astype(jnp.float32)]
    convert_element_type x4 -> x8, other arithmetic: 9.32 us -> 15 us  [scatter_sum(): up_block.astype(jnp.bfloat16)]
    another operation x0 -> x2, other arithmetic: none -> 4.49 us  [local(): return jnp.stack(outputs, axis=0)[None]]
  transfers between devices with their start and end apart: 31 -> 44, of which waited for: 9 -> 11; matrix products, arithmetic and copies ran while one was open for 3% -> 8% of each run, Pallas kernels for 14% -> 20%
where the time goes in v3:
time: 407 us; the launch traced here: 400 us
  starting transfers between devices  161 us (40%)
  Pallas kernels  143 us (35%)
  waiting for transfers between devices  46.1 us (11%)
  other arithmetic  37.9 us (9%)
  local copies, waits for them, and re-layouts  5.95 us (1%)
  matrix products  5.29 us (1%)
    ppermute x42, starting transfers between devices, send_on(): return lax.ppermute(value, ('pipe', axis), pairs_on(section, axis, links))  84.6 us
    pallas_call x8, Pallas kernels, project(): pl.pallas_call(functools.partial(project_kernel, base is not None, inv_rm...  80.1 us
    ppermute x2, starting transfers between devices, local(): streams = [lax.ppermute(first, 'pipe', [(0, 1)]) for first in firsts]  76.4 us
    ppermute x42, waiting for transfers between devices, send_on(): return lax.ppermute(value, ('pipe', axis), pairs_on(section, axis, links))  43.4 us
    pallas_call x4, Pallas kernels, out_product(): pl.pallas_call(out_kernel, grid=(count, per_block), in_specs=[pl.BlockSpe...  39.3 us
    pallas_call x4, Pallas kernels, mix(): pl.pallas_call(functools.partial(mix_kernel, taps.shape[0], history is no...  23.5 us
    convert_element_type x8, other arithmetic, scatter_sum(): up_block.astype(jnp.bfloat16)  15 us
  transfers between devices with their start and end apart: 44, of which 11 were waited for; matrix products, arithmetic and copies ran while one was open for 8% of the time, Pallas kernels for 20%

profile of v3, /device:TPU:25, one launch (start us, length us, event | category | flops | bytes accessed | tf_op | source)
XLA Modules:
  0.0 400.2 jit_solution(5209685970999997139)
XLA Ops:
  3.5 7.5 %shard_map.82.refs_0_ = f32[128,3072]{1,0:T(8,128)S(1)} custom-call(s32[1]{0:T(128)} %bitcast.5.owner_ref, bf16[144,2048]{1,0:T(8,128)(2,1)S(1)} %fusion.49.x_ref, bf16[3,8192,1024]{2,1,0:T(8,128)(2,1)} %bitcast.135, bf16[3,8192,1024]{2,1,0:T(8,128)(2,1)} %bitcast.136), custom_call_target="tpu_custom_call" | custom-call | flops 1610612736 | bytes 13107200 | tf_op jit(solution)/shard_map/pallas_call | solution.py:126
  12.6 7.5 %shard_map.83.refs_0_ = f32[128,3072]{1,0:T(8,128)S(1)} custom-call(s32[1]{0:T(128)} %bitcast.8.owner_ref, bf16[144,2048]{1,0:T(8,128)(2,1)S(1)} %broadcast_select_fusion.1.x_ref, bf16[3,8192,1024]{2,1,0:T(8,128)(2,1)} %bitcast.137, bf16[3,8192,1024]{2,1,0:T(8,128)(2,1)} %bitcast.138, f32[128,3072]{1,0:T(8,128)S(1)} %shard_map.82.refs_0_), custom_call_target="tpu_custom_call" | custom-call | flops 1610612736 | bytes 13107200 | tf_op jit(solution)/shard_map/pallas_call | solution.py:126
  21.8 7.5 %shard_map.84.refs_0_ = f32[128,3072]{1,0:T(8,128)S(1)} custom-call(s32[1]{0:T(128)} %bitcast.10.owner_ref, bf16[144,2048]{1,0:T(8,128)(2,1)S(1)} %select_select_fusion.3.x_ref, bf16[3,8192,1024]{2,1,0:T(8,128)(2,1)} %bitcast.139, bf16[3,8192,1024]{2,1,0:T(8,128)(2,1)} %bitcast.140, f32[128,3072]{1,0:T(8,128)S(1)} %shard_map.83.refs_0_), custom_call_target="tpu_custom_call" | custom-call | flops 1610612736 | bytes 13107200 | tf_op jit(solution)/shard_map/pallas_call | solution.py:126
  29.6 7.7 %shard_map.85 = bf16[128,3072]{1,0:T(8,128)(2,1)S(1)} custom-call(s32[1]{0:T(128)} %bitcast.2.owner_ref, bf16[144,2048]{1,0:T(8,128)(2,1)S(1)} %select_select_fusion.2.x_ref, bf16[3,8192,1024]{2,1,0:T(8,128)(2,1)} %bitcast.141, bf16[3,8192,1024]{2,1,0:T(8,128)(2,1)} %bitcast.142, f32[128,3072]{1,0:T(8,128)S(1)} %shard_map.84.refs_0_, f32[128,1]{1,0:T(8,128)S(1)} %copy.10.refs_1_), custom_call_target="tpu_custom_call" | custom-call | flops 1610612736 | bytes 13107200 | tf_op jit(solution)/shard_map/pallas_call | solution.py:126
  47.5 9.8 %shard_map.89 = bf16[4,192,2048]{2,1,0:T(8,128)(2,1)S(1)} custom-call(bf16[192,1024]{1,0:T(8,128)(2,1)S(1)} %bitcast.130, bf16[1024,8192]{1,0:T(8,128)(2,1)} %bitcast.151, bf16[1024,8192]{1,0:T(8,128)(2,1)} %bitcast.152), custom_call_target="tpu_custom_call" | custom-call | flops 3221225472 | bytes 19922944 | tf_op jit(solution)/shard_map/pallas_call | solution.py:195
  60.2 9.8 %shard_map.87 = bf16[4,192,2048]{2,1,0:T(8,128)(2,1)S(1)} custom-call(bf16[192,1024]{1,0:T(8,128)(2,1)S(1)} %bitcast.128, bf16[1024,8192]{1,0:T(8,128)(2,1)} %bitcast.153, bf16[1024,8192]{1,0:T(8,128)(2,1)} %bitcast.154), custom_call_target="tpu_custom_call" | custom-call | flops 3221225472 | bytes 19922944 | tf_op jit(solution)/shard_map/pallas_call | solution.py:195
  85.6 3.3 fusion.30
  90.4 3.2 fusion.37
  109.1 3.3 fusion.40
  112.4 69.3 %collective-permute-start.16 = (bf16[192,2048]{1,0:T(8,128)(2,1)S(1)}, bf16[192,2048]{1,0:T(8,128)(2,1)S(1)}, u32[]{:S(2)}, u32[]{:S(2)}) collective-permute-start(bf16[192,2048]{1,0:T(8,128)(2,1)S(1)} %get-tuple-element.65), channel_id=1, source_target_pairs={{0,16},{1,17},{2,18},{3,19},{4,20},{5,21},{6,22},{7,23},{8,24},{9,... | collective-permute-start | bytes 2359304 | tf_op jit(solution)/shard_map/ppermute | solution.py:347
  181.7 7.1 %collective-permute-start.23 = (bf16[192,2048]{1,0:T(8,128)(2,1)S(1)}, bf16[192,2048]{1,0:T(8,128)(2,1)S(1)}, u32[]{:S(2)}, u32[]{:S(2)}) collective-permute-start(bf16[192,2048]{1,0:T(8,128)(2,1)S(1)} %get-tuple-element.66), channel_id=1, source_target_pairs={{0,16},{1,17},{2,18},{3,19},{4,20},{5,21},{6,22},{7,23},{8,24},{9,... | collective-permute-start | bytes 2359304 | tf_op jit(solution)/shard_map/ppermute | solution.py:347
  196.0 12.0 %shard_map.90.refs_0_ = f32[384,3072]{1,0:T(8,128)} custom-call(s32[1]{0:T(128)} %bitcast.5.owner_ref, bf16[400,2048]{1,0:T(8,128)(2,1)S(1)} %fusion.12.x_ref, bf16[3,8192,1024]{2,1,0:T(8,128)(2,1)} %bitcast.143, bf16[3,8192,1024]{2,1,0:T(8,128)(2,1)} %bitcast.144), custom_call_target="tpu_custom_call" | custom-call | flops 4831838208 | bytes 14155776 | tf_op jit(solution)/shard_map/pallas_call | solution.py:126
  208.0 4.6 %collective-permute-done.25 = bf16[400,2048]{1,0:T(8,128)(2,1)S(1)} collective-permute-done((bf16[400,2048]{1,0:T(8,128)(2,1)S(1)}, bf16[400,2048]{1,0:T(8,128)(2,1)S(1)}, u32[]{:S(2)}, u32[]{:S(2)}) %collective-permute-start.25) | collective-permute-done | bytes 1638432 | tf_op jit(solution)/shard_map/ppermute | solution.py:28
  212.6 3.9 collective-permute-done.24
  218.8 12.9 %shard_map.91.refs_0_ = f32[384,3072]{1,0:T(8,128)} custom-call(s32[1]{0:T(128)} %bitcast.8.owner_ref, bf16[400,2048]{1,0:T(8,128)(2,1)S(1)} %broadcast_select_fusion.x_ref, bf16[3,8192,1024]{2,1,0:T(8,128)(2,1)} %bitcast.145, bf16[3,8192,1024]{2,1,0:T(8,128)(2,1)} %bitcast.146, f32[384,3072]{1,0:T(8,128)} %shard_map.90.refs_0_), custom_call_target="tpu_custom_call" | custom-call | flops 4831838208 | bytes 14155776 | tf_op jit(solution)/shard_map/pallas_call | solution.py:126
  231.7 6.7 %collective-permute-done.26 = bf16[400,2048]{1,0:T(8,128)(2,1)S(1)} collective-permute-done((bf16[400,2048]{1,0:T(8,128)(2,1)S(1)}, bf16[400,2048]{1,0:T(8,128)(2,1)S(1)}, u32[]{:S(2)}, u32[]{:S(2)}) %collective-permute-start.26) | collective-permute-done | bytes 1638432 | tf_op jit(solution)/shard_map/ppermute | solution.py:28
  240.7 12.8 %shard_map.92.refs_0_ = f32[384,3072]{1,0:T(8,128)} custom-call(s32[1]{0:T(128)} %bitcast.10.owner_ref, bf16[400,2048]{1,0:T(8,128)(2,1)S(1)} %select_select_fusion.1.x_ref, bf16[3,8192,1024]{2,1,0:T(8,128)(2,1)} %bitcast.147, bf16[3,8192,1024]{2,1,0:T(8,128)(2,1)} %bitcast.148, f32[384,3072]{1,0:T(8,128)} %shard_map.91.refs_0_), custom_call_target="tpu_custom_call" | custom-call | flops 4831838208 | bytes 14155776 | tf_op jit(solution)/shard_map/pallas_call | solution.py:126
  253.6 6.7 %collective-permute-done.28 = bf16[400,2048]{1,0:T(8,128)(2,1)S(1)} collective-permute-done((bf16[400,2048]{1,0:T(8,128)(2,1)S(1)}, bf16[400,2048]{1,0:T(8,128)(2,1)S(1)}, u32[]{:S(2)}, u32[]{:S(2)}) %collective-permute-start.28) | collective-permute-done | bytes 1638432 | tf_op jit(solution)/shard_map/ppermute | solution.py:28
  260.7 12.2 %shard_map.93 = bf16[384,3072]{1,0:T(8,128)(2,1)} custom-call(s32[1]{0:T(128)} %bitcast.2.owner_ref, bf16[400,2048]{1,0:T(8,128)(2,1)S(1)} %select_select_fusion.x_ref, bf16[3,8192,1024]{2,1,0:T(8,128)(2,1)} %bitcast.149, bf16[3,8192,1024]{2,1,0:T(8,128)(2,1)} %bitcast.150, f32[384,3072]{1,0:T(8,128)} %shard_map.92.refs_0_, f32[384,1]{1,0:T(8,128)S(1)} %reshape.375.refs_1_), custom_call_target="tpu_custom_call" | custom-call | flops 4831838208 | bytes 14155776 | tf_op jit(solution)/shard_map/pallas_call | solution.py:126
  275.4 7.6 %collective-permute-start.30 = (bf16[2,16,3072]{2,1,0:T(8,128)(2,1)S(1)}, bf16[2,16,3072]{2,1,0:T(8,128)(2,1)S(1)}, u32[]{:S(2)}, u32[]{:S(2)}) collective-permute-start(bf16[2,16,3072]{2,1,0:T(8,128)(2,1)S(1)} %slice.105), channel_id=1, source_target_pairs={{16,20},{20,24},{24,28},{28,16},{17,21},{21,25},{25,29},{29,17},{1... | collective-permute-start | bytes 589832 | tf_op jit(solution)/shard_map/ppermute | solution.py:28
  283.8 7.1 %collective-permute-start.31 = (bf16[2,128,1024]{2,1,0:T(8,128)(2,1)S(1)}, bf16[2,128,1024]{2,1,0:T(8,128)(2,1)S(1)}, u32[]{:S(2)}, u32[]{:S(2)}) collective-permute-start(bf16[2,128,1024]{2,1,0:T(8,128)(2,1)S(1)} %fusion.44), channel_id=1, source_target_pairs={{16,20},{20,24},{24,28},{28,16},{17,21},{21,25},{25,29},{29,17},{1... | collective-permute-start | bytes 1572872 | tf_op jit(solution)/shard_map/ppermute | solution.py:28
  291.2 8.2 %collective-permute-done.31 = bf16[2,128,1024]{2,1,0:T(8,128)(2,1)S(1)} collective-permute-done((bf16[2,128,1024]{2,1,0:T(8,128)(2,1)S(1)}, bf16[2,128,1024]{2,1,0:T(8,128)(2,1)S(1)}, u32[]{:S(2)}, u32[]{:S(2)}) %collective-permute-start.31) | collective-permute-done | bytes 524320 | tf_op jit(solution)/shard_map/ppermute | solution.py:28
  299.5 10.0 %shard_map.96 = bf16[1,192,1024]{2,1,0:T(8,128)(2,1)S(1)} custom-call(bf16[2,208,3072]{2,1,0:T(8,128)(2,1)S(1)} %pad_maximum_fusion.refs_0_.refs_1_.refs_2_, bf16[2,208,3072]{2,1,0:T(8,128)(2,1)S(1)} %pad_maximum_fusion.refs_0_.refs_1_.refs_2_, bf16[2,208,3072]{2,1,0:T(8,128)(2,1)S(1)} %pad_maximum_fusion.refs_0_.refs_1_.refs_2_, ...), custom_call_target="tpu_custom_call" | custom-call | flops 50331648 | bytes 1703936 | tf_op jit(solution)/shard_map/pallas_call | solution.py:282
  309.5 10.0 %shard_map.94 = bf16[1,192,1024]{2,1,0:T(8,128)(2,1)S(1)} custom-call(bf16[2,208,3072]{2,1,0:T(8,128)(2,1)S(1)} %pad_maximum_fusion.refs_0_.refs_1_.refs_2_, bf16[2,208,3072]{2,1,0:T(8,128)(2,1)S(1)} %pad_maximum_fusion.refs_0_.refs_1_.refs_2_, bf16[2,208,3072]{2,1,0:T(8,128)(2,1)S(1)} %pad_maximum_fusion.refs_0_.refs_1_.refs_2_, ...), custom_call_target="tpu_custom_call" | custom-call | flops 50331648 | bytes 1703936 | tf_op jit(solution)/shard_map/pallas_call | solution.py:282
  319.5 9.8 %shard_map.97 = bf16[4,192,2048]{2,1,0:T(8,128)(2,1)S(1)} custom-call(bf16[192,1024]{1,0:T(8,128)(2,1)S(1)} %bitcast.129, bf16[1024,8192]{1,0:T(8,128)(2,1)} %bitcast.155, bf16[1024,8192]{1,0:T(8,128)(2,1)} %bitcast.156), custom_call_target="tpu_custom_call" | custom-call | flops 3221225472 | bytes 19922944 | tf_op jit(solution)/shard_map/pallas_call | solution.py:195
  330.2 9.9 %shard_map.95 = bf16[4,192,2048]{2,1,0:T(8,128)(2,1)S(1)} custom-call(bf16[192,1024]{1,0:T(8,128)(2,1)S(1)} %bitcast.127, bf16[1024,8192]{1,0:T(8,128)(2,1)} %bitcast.157, bf16[1024,8192]{1,0:T(8,128)(2,1)} %bitcast.158), custom_call_target="tpu_custom_call" | custom-call | flops 3221225472 | bytes 19922944 | tf_op jit(solution)/shard_map/pallas_call | solution.py:195
  347.1 5.0 %collective-permute-done.41 = bf16[192,2048]{1,0:T(8,128)(2,1)S(1)} collective-permute-done((bf16[192,2048]{1,0:T(8,128)(2,1)S(1)}, bf16[192,2048]{1,0:T(8,128)(2,1)S(1)}, u32[]{:S(2)}, u32[]{:S(2)}) %collective-permute-start.41) | collective-permute-done | bytes 786464 | tf_op jit(solution)/shard_map/ppermute | solution.py:28
  353.7 5.4 %collective-permute-start.42 = (bf16[192,2048]{1,0:T(8,128)(2,1)S(1)}, bf16[192,2048]{1,0:T(8,128)(2,1)S(1)}, u32[]{:S(2)}, u32[]{:S(2)}) collective-permute-start(bf16[192,2048]{1,0:T(8,128)(2,1)S(1)} %get-tuple-element.50), channel_id=1, source_target_pairs={{18,17},{19,18},{22,21},{23,22},{26,25},{27,26},{30,29},{31,30}} | collective-permute-start | bytes 2359304 | tf_op jit(solution)/shard_map/ppermute | solution.py:28
  362.0 7.4 %collective-permute-start.36 = (bf16[192,2048]{1,0:T(8,128)(2,1)S(1)}, bf16[192,2048]{1,0:T(8,128)(2,1)S(1)}, u32[]{:S(2)}, u32[]{:S(2)}) collective-permute-start(bf16[192,2048]{1,0:T(8,128)(2,1)S(1)} %get-tuple-element.46), channel_id=1, source_target_pairs={{18,17},{19,18},{22,21},{23,22},{26,25},{27,26},{30,29},{31,30}} | collective-permute-start | bytes 2359304 | tf_op jit(solution)/shard_map/ppermute | solution.py:28
  371.9 8.2 %collective-permute-start.43 = (bf16[192,2048]{1,0:T(8,128)(2,1)}, bf16[192,2048]{1,0:T(8,128)(2,1)}, u32[]{:S(2)}, u32[]{:S(2)}) collective-permute-start(bf16[192,2048]{1,0:T(8,128)(2,1)} %fusion.14), channel_id=1, source_target_pairs={{17,16},{18,17},{19,18},{21,20},{22,21},{23,22},{25,24},{26,25},{2... | collective-permute-start | bytes 2359304 | tf_op jit(solution)/shard_map/ppermute | solution.py:28
  382.7 4.9 %collective-permute-start.37 = (bf16[192,2048]{1,0:T(8,128)(2,1)}, bf16[192,2048]{1,0:T(8,128)(2,1)}, u32[]{:S(2)}, u32[]{:S(2)}) collective-permute-start(bf16[192,2048]{1,0:T(8,128)(2,1)} %fusion.21), channel_id=1, source_target_pairs={{17,16},{18,17},{19,18},{21,20},{22,21},{23,22},{25,24},{26,25},{2... | collective-permute-start | bytes 2359304 | tf_op jit(solution)/shard_map/ppermute | solution.py:28
  391.0 3.3 collective-permute-done.34
  (170 shorter events, 94.5 us)
Async XLA Ops:
  2.1 9.0 %collective-permute-start.2 = (bf16[144,2048]{1,0:T(8,128)(2,1)S(1)}, bf16[144,2048]{1,0:T(8,128)(2,1)S(1)}, u32[]{:S(2)}, u32[]{:S(2)}) collective-permute-start(bf16[144,2048]{1,0:T(8,128)(2,1)S(1)} %fusion.49.x_ref), channel_id=1, source_target_pairs={{1,0},{2,1},{3,2},{5,4},{6,5},{7,6},{9,8},{10,9},{11,10},{13,12},{... | collective-permute-start | bytes 1769480 | tf_op jit(solution)/shard_map/ppermute | solution.py:28
  11.1 9.1 %collective-permute-start.3 = (bf16[144,2048]{1,0:T(8,128)(2,1)S(1)}, bf16[144,2048]{1,0:T(8,128)(2,1)S(1)}, u32[]{:S(2)}, u32[]{:S(2)}) collective-permute-start(bf16[144,2048]{1,0:T(8,128)(2,1)S(1)} %collective-permute-done.1), channel_id=1, source_target_pairs={{1,2},{2,3},{5,6},{6,7},{9,10},{10,11},{13,14},{14,15}} | collective-permute-start | bytes 1769480 | tf_op jit(solution)/shard_map/ppermute | solution.py:28
  20.2 9.1 %collective-permute-start.5 = (bf16[144,2048]{1,0:T(8,128)(2,1)S(1)}, bf16[144,2048]{1,0:T(8,128)(2,1)S(1)}, u32[]{:S(2)}, u32[]{:S(2)}) collective-permute-start(bf16[144,2048]{1,0:T(8,128)(2,1)S(1)} %collective-permute-done.3), channel_id=1, source_target_pairs={{2,3},{6,7},{10,11},{14,15}} | collective-permute-start | bytes 1769480 | tf_op jit(solution)/shard_map/ppermute | solution.py:28
  58.5 17.4 %collective-permute-start.17 = (bf16[192,2048]{1,0:T(8,128)(2,1)}, bf16[192,2048]{1,0:T(8,128)(2,1)}, u32[]{:S(2)}, u32[]{:S(2)}) collective-permute-start(bf16[192,2048]{1,0:T(8,128)(2,1)} %get-tuple-element.59), channel_id=1, source_target_pairs={{0,1},{4,5},{8,9},{12,13}} | collective-permute-start | bytes 2359304 | tf_op jit(solution)/shard_map/ppermute | solution.py:28
  72.8 8.6 %collective-permute-start.10 = (bf16[192,2048]{1,0:T(8,128)(2,1)}, bf16[192,2048]{1,0:T(8,128)(2,1)}, u32[]{:S(2)}, u32[]{:S(2)}) collective-permute-start(bf16[192,2048]{1,0:T(8,128)(2,1)} %get-tuple-element.55), channel_id=1, source_target_pairs={{0,1},{4,5},{8,9},{12,13}} | collective-permute-start | bytes 2359304 | tf_op jit(solution)/shard_map/ppermute | solution.py:28
  74.4 11.2 %collective-permute-start.20 = (bf16[192,2048]{1,0:T(8,128)(2,1)}, bf16[192,2048]{1,0:T(8,128)(2,1)}, u32[]{:S(2)}, u32[]{:S(2)}) collective-permute-start(bf16[192,2048]{1,0:T(8,128)(2,1)} %get-tuple-element.60), channel_id=1, source_target_pairs={{3,2},{7,6},{11,10},{15,14}} | collective-permute-start | bytes 2359304 | tf_op jit(solution)/shard_map/ppermute | solution.py:28
  79.9 10.6 %collective-permute-start.13 = (bf16[192,2048]{1,0:T(8,128)(2,1)}, bf16[192,2048]{1,0:T(8,128)(2,1)}, u32[]{:S(2)}, u32[]{:S(2)}) collective-permute-start(bf16[192,2048]{1,0:T(8,128)(2,1)} %get-tuple-element.56), channel_id=1, source_target_pairs={{3,2},{7,6},{11,10},{15,14}} | collective-permute-start | bytes 2359304 | tf_op jit(solution)/shard_map/ppermute | solution.py:28
  88.9 9.5 %collective-permute-start.21 = (bf16[192,2048]{1,0:T(8,128)(2,1)}, bf16[192,2048]{1,0:T(8,128)(2,1)}, u32[]{:S(2)}, u32[]{:S(2)}) collective-permute-start(bf16[192,2048]{1,0:T(8,128)(2,1)} %get-tuple-element.58), channel_id=1, source_target_pairs={{2,1},{3,2},{6,5},{7,6},{10,9},{11,10},{14,13},{15,14}} | collective-permute-start | bytes 2359304 | tf_op jit(solution)/shard_map/ppermute | solution.py:28
  93.7 8.6 %collective-permute-start.14 = (bf16[192,2048]{1,0:T(8,128)(2,1)}, bf16[192,2048]{1,0:T(8,128)(2,1)}, u32[]{:S(2)}, u32[]{:S(2)}) collective-permute-start(bf16[192,2048]{1,0:T(8,128)(2,1)} %get-tuple-element.54), channel_id=1, source_target_pairs={{2,1},{3,2},{6,5},{7,6},{10,9},{11,10},{14,13},{15,14}} | collective-permute-start | bytes 2359304 | tf_op jit(solution)/shard_map/ppermute | solution.py:28
  95.3 13.8 %collective-permute-start.19 = (bf16[192,2048]{1,0:T(8,128)(2,1)}, bf16[192,2048]{1,0:T(8,128)(2,1)}, u32[]{:S(2)}, u32[]{:S(2)}) collective-permute-start(bf16[192,2048]{1,0:T(8,128)(2,1)} %get-tuple-element.57), channel_id=1, source_target_pairs={{0,1},{1,2},{2,3},{4,5},{5,6},{6,7},{8,9},{9,10},{10,11},{12,13},{... | collective-permute-start | bytes 2359304 | tf_op jit(solution)/shard_map/ppermute | solution.py:28
  96.9 12.2 %collective-permute-start.12 = (bf16[192,2048]{1,0:T(8,128)(2,1)}, bf16[192,2048]{1,0:T(8,128)(2,1)}, u32[]{:S(2)}, u32[]{:S(2)}) collective-permute-start(bf16[192,2048]{1,0:T(8,128)(2,1)} %get-tuple-element.53), channel_id=1, source_target_pairs={{0,1},{1,2},{2,3},{4,5},{5,6},{6,7},{8,9},{9,10},{10,11},{12,13},{... | collective-permute-start | bytes 2359304 | tf_op jit(solution)/shard_map/ppermute | solution.py:28
  112.4 76.4 %collective-permute-start.16 = (bf16[192,2048]{1,0:T(8,128)(2,1)S(1)}, bf16[192,2048]{1,0:T(8,128)(2,1)S(1)}, u32[]{:S(2)}, u32[]{:S(2)}) collective-permute-start(bf16[192,2048]{1,0:T(8,128)(2,1)S(1)} %get-tuple-element.65), channel_id=1, source_target_pairs={{0,16},{1,17},{2,18},{3,19},{4,20},{5,21},{6,22},{7,23},{8,24},{9,... | collective-permute-start | bytes 2359304 | tf_op jit(solution)/shard_map/ppermute | solution.py:347
  181.7 9.8 %collective-permute-start.23 = (bf16[192,2048]{1,0:T(8,128)(2,1)S(1)}, bf16[192,2048]{1,0:T(8,128)(2,1)S(1)}, u32[]{:S(2)}, u32[]{:S(2)}) collective-permute-start(bf16[192,2048]{1,0:T(8,128)(2,1)S(1)} %get-tuple-element.66), channel_id=1, source_target_pairs={{0,16},{1,17},{2,18},{3,19},{4,20},{5,21},{6,22},{7,23},{8,24},{9,... | collective-permute-start | bytes 2359304 | tf_op jit(solution)/shard_map/ppermute | solution.py:347
  192.5 20.2 %collective-permute-start.25 = (bf16[400,2048]{1,0:T(8,128)(2,1)S(1)}, bf16[400,2048]{1,0:T(8,128)(2,1)S(1)}, u32[]{:S(2)}, u32[]{:S(2)}) collective-permute-start(bf16[400,2048]{1,0:T(8,128)(2,1)S(1)} %fusion.12.x_ref), channel_id=1, source_target_pairs={{17,16},{18,17},{19,18},{21,20},{22,21},{23,22},{25,24},{26,25},{2... | collective-permute-start | bytes 4915208 | tf_op jit(solution)/shard_map/ppermute | solution.py:28
  194.7 21.9 %collective-permute-start.24 = (bf16[400,2048]{1,0:T(8,128)(2,1)S(1)}, bf16[400,2048]{1,0:T(8,128)(2,1)S(1)}, u32[]{:S(2)}, u32[]{:S(2)}) collective-permute-start(bf16[400,2048]{1,0:T(8,128)(2,1)S(1)} %fusion.12.x_ref), channel_id=1, source_target_pairs={{16,17},{17,18},{18,19},{20,21},{21,22},{22,23},{24,25},{25,26},{2... | collective-permute-start | bytes 4915208 | tf_op jit(solution)/shard_map/ppermute | solution.py:28
  216.6 21.9 %collective-permute-start.26 = (bf16[400,2048]{1,0:T(8,128)(2,1)S(1)}, bf16[400,2048]{1,0:T(8,128)(2,1)S(1)}, u32[]{:S(2)}, u32[]{:S(2)}) collective-permute-start(bf16[400,2048]{1,0:T(8,128)(2,1)S(1)} %collective-permute-done.24), channel_id=1, source_target_pairs={{17,18},{18,19},{21,22},{22,23},{25,26},{26,27},{29,30},{30,31}} | collective-permute-start | bytes 4915208 | tf_op jit(solution)/shard_map/ppermute | solution.py:28
  217.8 20.6 %collective-permute-start.27 = (bf16[400,2048]{1,0:T(8,128)(2,1)S(1)}, bf16[400,2048]{1,0:T(8,128)(2,1)S(1)}, u32[]{:S(2)}, u32[]{:S(2)}) collective-permute-start(bf16[400,2048]{1,0:T(8,128)(2,1)S(1)} %collective-permute-done.25), channel_id=1, source_target_pairs={{17,16},{18,17},{21,20},{22,21},{25,24},{26,25},{29,28},{30,29}} | collective-permute-start | bytes 4915208 | tf_op jit(solution)/shard_map/ppermute | solution.py:28
  238.4 21.9 %collective-permute-start.28 = (bf16[400,2048]{1,0:T(8,128)(2,1)S(1)}, bf16[400,2048]{1,0:T(8,128)(2,1)S(1)}, u32[]{:S(2)}, u32[]{:S(2)}) collective-permute-start(bf16[400,2048]{1,0:T(8,128)(2,1)S(1)} %collective-permute-done.26), channel_id=1, source_target_pairs={{18,19},{22,23},{26,27},{30,31}} | collective-permute-start | bytes 4915208 | tf_op jit(solution)/shard_map/ppermute | solution.py:28
  239.7 20.6 %collective-permute-start.29 = (bf16[400,2048]{1,0:T(8,128)(2,1)S(1)}, bf16[400,2048]{1,0:T(8,128)(2,1)S(1)}, u32[]{:S(2)}, u32[]{:S(2)}) collective-permute-start(bf16[400,2048]{1,0:T(8,128)(2,1)S(1)} %collective-permute-done.27), channel_id=1, source_target_pairs={{17,16},{21,20},{25,24},{29,28}} | collective-permute-start | bytes 4915208 | tf_op jit(solution)/shard_map/ppermute | solution.py:28
  275.4 15.5 %collective-permute-start.30 = (bf16[2,16,3072]{2,1,0:T(8,128)(2,1)S(1)}, bf16[2,16,3072]{2,1,0:T(8,128)(2,1)S(1)}, u32[]{:S(2)}, u32[]{:S(2)}) collective-permute-start(bf16[2,16,3072]{2,1,0:T(8,128)(2,1)S(1)} %slice.105), channel_id=1, source_target_pairs={{16,20},{20,24},{24,28},{28,16},{17,21},{21,25},{25,29},{29,17},{1... | collective-permute-start | bytes 589832 | tf_op jit(solution)/shard_map/ppermute | solution.py:28
  283.8 15.6 %collective-permute-start.31 = (bf16[2,128,1024]{2,1,0:T(8,128)(2,1)S(1)}, bf16[2,128,1024]{2,1,0:T(8,128)(2,1)S(1)}, u32[]{:S(2)}, u32[]{:S(2)}) collective-permute-start(bf16[2,128,1024]{2,1,0:T(8,128)(2,1)S(1)} %fusion.44), channel_id=1, source_target_pairs={{16,20},{20,24},{24,28},{28,16},{17,21},{21,25},{25,29},{29,17},{1... | collective-permute-start | bytes 1572872 | tf_op jit(solution)/shard_map/ppermute | solution.py:28
  329.5 13.7 %collective-permute-start.38 = (bf16[192,2048]{1,0:T(8,128)(2,1)S(1)}, bf16[192,2048]{1,0:T(8,128)(2,1)S(1)}, u32[]{:S(2)}, u32[]{:S(2)}) collective-permute-start(bf16[192,2048]{1,0:T(8,128)(2,1)S(1)} %get-tuple-element.51), channel_id=1, source_target_pairs={{16,17},{20,21},{24,25},{28,29}} | collective-permute-start | bytes 2359304 | tf_op jit(solution)/shard_map/ppermute | solution.py:28
  341.0 11.0 %collective-permute-start.41 = (bf16[192,2048]{1,0:T(8,128)(2,1)S(1)}, bf16[192,2048]{1,0:T(8,128)(2,1)S(1)}, u32[]{:S(2)}, u32[]{:S(2)}) collective-permute-start(bf16[192,2048]{1,0:T(8,128)(2,1)S(1)} %get-tuple-element.52), channel_id=1, source_target_pairs={{19,18},{23,22},{27,26},{31,30}} | collective-permute-start | bytes 2359304 | tf_op jit(solution)/shard_map/ppermute | solution.py:28
  343.5 8.6 %collective-permute-start.39 = (bf16[192,2048]{1,0:T(8,128)(2,1)S(1)}, bf16[192,2048]{1,0:T(8,128)(2,1)S(1)}, u32[]{:S(2)}, u32[]{:S(2)}) collective-permute-start(bf16[192,2048]{1,0:T(8,128)(2,1)S(1)} %fusion.15), channel_id=1, source_target_pairs={{16,17},{17,18},{20,21},{21,22},{24,25},{25,26},{28,29},{29,30}} | collective-permute-start | bytes 2359304 | tf_op jit(solution)/shard_map/ppermute | solution.py:28
  344.2 16.3 %collective-permute-start.35 = (bf16[192,2048]{1,0:T(8,128)(2,1)S(1)}, bf16[192,2048]{1,0:T(8,128)(2,1)S(1)}, u32[]{:S(2)}, u32[]{:S(2)}) collective-permute-start(bf16[192,2048]{1,0:T(8,128)(2,1)S(1)} %get-tuple-element.48), channel_id=1, source_target_pairs={{19,18},{23,22},{27,26},{31,30}} | collective-permute-start | bytes 2359304 | tf_op jit(solution)/shard_map/ppermute | solution.py:28
  346.4 14.1 %collective-permute-start.33 = (bf16[192,2048]{1,0:T(8,128)(2,1)S(1)}, bf16[192,2048]{1,0:T(8,128)(2,1)S(1)}, u32[]{:S(2)}, u32[]{:S(2)}) collective-permute-start(bf16[192,2048]{1,0:T(8,128)(2,1)S(1)} %fusion.22), channel_id=1, source_target_pairs={{16,17},{17,18},{20,21},{21,22},{24,25},{25,26},{28,29},{29,30}} | collective-permute-start | bytes 2359304 | tf_op jit(solution)/shard_map/ppermute | solution.py:28
  353.7 17.0 %collective-permute-start.42 = (bf16[192,2048]{1,0:T(8,128)(2,1)S(1)}, bf16[192,2048]{1,0:T(8,128)(2,1)S(1)}, u32[]{:S(2)}, u32[]{:S(2)}) collective-permute-start(bf16[192,2048]{1,0:T(8,128)(2,1)S(1)} %get-tuple-element.50), channel_id=1, source_target_pairs={{18,17},{19,18},{22,21},{23,22},{26,25},{27,26},{30,29},{31,30}} | collective-permute-start | bytes 2359304 | tf_op jit(solution)/shard_map/ppermute | solution.py:28
  362.0 19.5 %collective-permute-start.36 = (bf16[192,2048]{1,0:T(8,128)(2,1)S(1)}, bf16[192,2048]{1,0:T(8,128)(2,1)S(1)}, u32[]{:S(2)}, u32[]{:S(2)}) collective-permute-start(bf16[192,2048]{1,0:T(8,128)(2,1)S(1)} %get-tuple-element.46), channel_id=1, source_target_pairs={{18,17},{19,18},{22,21},{23,22},{26,25},{27,26},{30,29},{31,30}} | collective-permute-start | bytes 2359304 | tf_op jit(solution)/shard_map/ppermute | solution.py:28
  369.4 18.2 %collective-permute-start.40 = (bf16[192,2048]{1,0:T(8,128)(2,1)}, bf16[192,2048]{1,0:T(8,128)(2,1)}, u32[]{:S(2)}, u32[]{:S(2)}) collective-permute-start(bf16[192,2048]{1,0:T(8,128)(2,1)} %get-tuple-element.49), channel_id=1, source_target_pairs={{16,17},{17,18},{18,19},{20,21},{21,22},{22,23},{24,25},{25,26},{2... | collective-permute-start | bytes 2359304 | tf_op jit(solution)/shard_map/ppermute | solution.py:28
  371.9 16.6 %collective-permute-start.43 = (bf16[192,2048]{1,0:T(8,128)(2,1)}, bf16[192,2048]{1,0:T(8,128)(2,1)}, u32[]{:S(2)}, u32[]{:S(2)}) collective-permute-start(bf16[192,2048]{1,0:T(8,128)(2,1)} %fusion.14), channel_id=1, source_target_pairs={{17,16},{18,17},{19,18},{21,20},{22,21},{23,22},{25,24},{26,25},{2... | collective-permute-start | bytes 2359304 | tf_op jit(solution)/shard_map/ppermute | solution.py:28
  380.1 14.1 %collective-permute-start.34 = (bf16[192,2048]{1,0:T(8,128)(2,1)}, bf16[192,2048]{1,0:T(8,128)(2,1)}, u32[]{:S(2)}, u32[]{:S(2)}) collective-permute-start(bf16[192,2048]{1,0:T(8,128)(2,1)} %get-tuple-element.45), channel_id=1, source_target_pairs={{16,17},{17,18},{18,19},{20,21},{21,22},{22,23},{24,25},{25,26},{2... | collective-permute-start | bytes 2359304 | tf_op jit(solution)/shard_map/ppermute | solution.py:28
  382.7 14.2 %collective-permute-start.37 = (bf16[192,2048]{1,0:T(8,128)(2,1)}, bf16[192,2048]{1,0:T(8,128)(2,1)}, u32[]{:S(2)}, u32[]{:S(2)}) collective-permute-start(bf16[192,2048]{1,0:T(8,128)(2,1)} %fusion.21), channel_id=1, source_target_pairs={{17,16},{18,17},{19,18},{21,20},{22,21},{23,22},{25,24},{26,25},{2... | collective-permute-start | bytes 2359304 | tf_op jit(solution)/shard_map/ppermute | solution.py:28
  (30 other events, 435.6 us)
